TPU v7x, 32 devices: a whole 2x2x4 slice. The times are simulated.
32 devices in a mesh: tm: 4 (over z), space: 8 (over y, x, core).
Axes of the slice: x: 2, y: 2, z: 4, core: 2. Of those that a mesh axis runs over, the one named last changes fastest.
Arguments:
- forcing: float32 [64, 3, 16, 8, 128], P('tm', None, 'space'), may hold values from -6 to 6
- start_field: float32 [3, 16, 8, 128], P(None, 'space'), may hold values from -6 to 6
- iterate: float32 [64, 3, 16, 8, 128], P('tm', None, 'space'), may hold values from -12 to 12
- region: int32 [16, 8, 128], P('space'), may hold values from 0 to 2
- conductance: float32 [3], replicated, may hold values from 0.5 to 4
Outputs:
- updated: float32 [64, 3, 16, 8, 128], P('tm', None, 'space')
All inputs are finite; a program needn't handle non-finite values.
Results may differ from a plain program's by a relative error of at most 0.00013.
Values sent between devices are 32-bit elements; how exact they have to be, the bound alone decides.
A program may use at most 64 MiB of HBM per device.

v0:
```python
import math

import jax
import jax.numpy as jnp
from jax import lax
from jax.sharding import PartitionSpec as P

SWEEPS = 12


ALPHA = 0.1
LOWER = 0.02
UPPER = 1.0
SIGMA_TOP = 4.0
CURL_TOP = 12.0


def from_behind(value, axis, steps):
    count = lax.axis_size(axis)
    initial, last = (max(0, -steps), min(count, count - steps))
    return lax.ppermute(value, axis, [(source, source + steps) for source in range(initial, last)])


def broadcast(array, axis, root):
    mine = lax.axis_index(axis) == root
    return lax.psum(jnp.where(mine, array, jnp.zeros_like(array)), axis)


def forward_step(values, axis):
    inner = lax.slice_in_dim(values, 1, values.shape[axis], axis=axis)
    border = jnp.zeros_like(lax.slice_in_dim(values, 0, 1, axis=axis))
    return jnp.concatenate([inner, border], axis) - values


def backward_step(values, axis):
    inner = lax.slice_in_dim(values, 0, values.shape[axis] - 1, axis=axis)
    border = jnp.zeros_like(lax.slice_in_dim(values, 0, 1, axis=axis))
    return jnp.concatenate([border, inner], axis) - values


def curl_forward(field):
    field_x, field_y, field_z = (field[:, 0], field[:, 1], field[:, 2])
    lead_x, lead_y, lead_z = (field_x[:, :-1], field_y[:, :-1], field_z[:, :-1])
    flux_x = forward_step(lead_z, 2) - forward_step(lead_y, 3)
    flux_y = forward_step(lead_x, 3) - (field_z[:, 1:] - field_z[:, :-1])
    flux_z = field_y[:, 1:] - field_y[:, :-1] - forward_step(lead_x, 2)
    return jnp.stack([flux_x, flux_y, flux_z], axis=1)


def curl_adjoint(flux):
    flux_x, flux_y, flux_z = (flux[:, 0], flux[:, 1], flux[:, 2])
    tail_x, tail_y, tail_z = (flux_x[:, 1:], flux_y[:, 1:], flux_z[:, 1:])
    field_x = backward_step(tail_y, 3) - backward_step(tail_z, 2)
    field_y = flux_z[:, :-1] - flux_z[:, 1:] - backward_step(tail_x, 3)
    field_z = backward_step(tail_x, 2) - (flux_y[:, :-1] - flux_y[:, 1:])
    return jnp.stack([field_x, field_y, field_z], axis=1)


def brick_curl(field):
    upper = from_behind(field[:, :, :1], "space", -1)
    flux = curl_forward(jnp.concatenate([field, upper], 2))
    lower = from_behind(flux[:, :, -1:], "space", 1)
    return curl_adjoint(jnp.concatenate([lower, flux], 2))


def pair_terms(pairs, window):
    gamma = ALPHA ** (1.0 / window)
    angle = 2.0 * math.pi * pairs.astype(jnp.float32) / window
    plain = 1.0 - gamma * jnp.cos(angle)
    p_plus = jnp.where(pairs == 0, 1.0 - gamma, plain)
    p_minus = jnp.where(pairs == 0, 1.0 + gamma, plain)
    q_term = jnp.where(pairs == 0, 0.0, gamma * jnp.sin(angle))
    bound = jnp.sqrt(jnp.maximum(p_plus, p_minus) ** 2 + q_term**2) * SIGMA_TOP + CURL_TOP
    return (p_plus, p_minus, q_term, bound * bound)


def cas_table(freqs, window):
    moments = jnp.arange(window)
    product = freqs[:, None] * moments[None, :] % window
    angle = 2.0 * math.pi * product.astype(jnp.float32) / window
    return jnp.cos(angle) + jnp.sin(angle)


def powers(window, sign):
    gamma = jnp.float32(ALPHA ** (sign / window))
    return jnp.power(gamma, jnp.arange(window).astype(jnp.float32))


def frequency_order(window, steps):
    slots = jnp.arange(window)
    half = steps // 2
    within = slots % steps
    pairs = slots // steps * half + within % half
    mirror = jnp.where(pairs == 0, window // 2, window - pairs)
    return jnp.where(within < half, pairs, mirror)


def chebyshev_terms(count):
    center = (UPPER + LOWER) / 2.0
    radius = (UPPER - LOWER) / 2.0
    spread_ratio = center / radius
    weight_now = 1.0 / spread_ratio
    carry_terms, push_terms = ([], [])
    for _ in range(count):
        weight_next = 1.0 / (2.0 * spread_ratio - weight_now)
        carry_terms.append(weight_next * weight_now)
        push_terms.append(2.0 * weight_next / radius)
        weight_now = weight_next
    return (jnp.asarray(carry_terms, jnp.float32), jnp.asarray(push_terms, jnp.float32), center)


def per_device(forcing, start_field, iterate, region, conductance):
    steps = forcing.shape[0]
    half = steps // 2
    groups = lax.axis_size("tm")
    window = steps * groups
    depth_z = forcing.shape[4]
    sigma = jnp.zeros(region.shape, jnp.float32)
    for material in range(3):
        sigma = sigma + conductance[material] * (region == material).astype(jnp.float32)
    order = frequency_order(window, steps)
    forward_table = cas_table(order, window) * powers(window, 1.0)[None, :]
    inverse_table = cas_table(order, window).T * (powers(window, -1.0) / window)[:, None]
    flat = forcing.reshape(steps, groups, -1, depth_z)
    spread = jnp.einsum(
        "kn,ngrz->kgrz",
        forward_table,
        lax.all_to_all(flat, "tm", split_axis=1, concat_axis=0, tiled=True),
        precision=lax.Precision.HIGHEST,
    )
    spectrum = lax.all_to_all(spread, "tm", split_axis=0, concat_axis=1, tiled=True).reshape(
        forcing.shape
    )
    latest = broadcast(iterate[steps - 1], "tm", lax.axis_size("tm") - 1)
    spectrum = spectrum + (sigma * (start_field - ALPHA * latest))[None]
    pairs = lax.axis_index("tm") * half + jnp.arange(half)
    p_plus, p_minus, q_term, scale = pair_terms(pairs, window)
    diagonal_coef = jnp.concatenate([p_plus, p_minus]).reshape(steps, 1, 1, 1, 1)
    cross = q_term.reshape(half, 1, 1, 1, 1)
    norm_scale = jnp.concatenate([scale, scale]).reshape(steps, 1, 1, 1, 1)

    def couple(values, sign, weights):
        swapped = jnp.concatenate([-cross * values[half:], cross * values[:half]], 0)
        return weights * (diagonal_coef * values + sign * swapped)

    def normal(values):
        first = brick_curl(values) + couple(values, 1.0, sigma)
        return (brick_curl(first) + couple(first, -1.0, sigma)) / norm_scale

    start = (brick_curl(spectrum) + couple(spectrum, -1.0, sigma)) / norm_scale
    carry_terms, push_terms, center = chebyshev_terms(SWEEPS - 1)

    def sweep(sweep_index, carry_state):
        current, residual, direction = carry_state
        current = current + direction
        residual = residual - normal(direction)
        direction = carry_terms[sweep_index] * direction + push_terms[sweep_index] * residual
        return (current, residual, direction)

    current, residual, direction = lax.fori_loop(
        0, SWEEPS - 1, sweep, (jnp.zeros_like(start), start, start / center)
    )
    solution = (current + direction).reshape(steps, groups, -1, depth_z)
    spread_back = jnp.einsum(
        "nk,kgrz->ngrz",
        inverse_table,
        lax.all_to_all(solution, "tm", split_axis=1, concat_axis=0, tiled=True),
        precision=lax.Precision.HIGHEST,
    )
    updated = lax.all_to_all(spread_back, "tm", split_axis=0, concat_axis=1, tiled=True)
    return updated.reshape(forcing.shape)


def solution(mesh):
    placed = (
        P("tm", None, "space", None, None),
        P(None, "space", None, None),
        P("tm", None, "space", None, None),
        P("space", None, None),
        P(),
    )
    return jax.shard_map(
        per_device,
        mesh=mesh,
        in_specs=placed,
        out_specs=P("tm", None, "space", None, None),
        check_vma=False,
    )
```

profile of v0, /device:TPU:0, one launch (start us, length us, event | category | flops | bytes accessed | tf_op | source)
XLA Modules:
  0.0 414.8 jit_solution(3538821860245970787)
XLA Ops:
  9.1 10.8 %all-to-all-done = f32[16,4,12,128]{3,0,2,1:T(8,128)S(1)} async-done(((f32[16,4,12,128]{3,0,2,1:T(8,128)}), f32[16,4,12,128]{3,0,2,1:T(8,128)S(1)}, u32[]{:S(2)}, u32[]{:S(2)}) %all-to-all-start) | async-done | bytes 393248 | tf_op jit(solution)/shard_map/all_to_all | solution.py:128
  25.3 19.6 %psum.7 = f32[3,2,8,128]{3,2,1,0:T(8,128)S(1)} all-reduce(f32[3,2,8,128]{3,2,1,0:T(8,128)S(1)} %select_bitcast_fusion), channel_id=1, replica_groups=mesh['tm'=4,'space'=8] {'tm'}, use_global_device_ids=true, to_apply=%region_0.1 | all-reduce | flops 6144 | bytes 49152 | tf_op jit(solution)/shard_map/psum | solution.py:26
  59.2 321.7 %while.22 = (s32[]{:T(128)}, f32[16,3,2,8,128]{4,3,2,1,0:T(8,128)S(1)}, f32[16,3,2,8,128]{4,3,2,1,0:T(8,128)S(1)}, f32[16,3,2,8,128]{4,3,2,1,0:T(8,128)S(1)}, f3...) while((s32[]{:T(128)}, ...), condition=%wide.region_2.3_spmd.clone.clone.clone.clone, body=%wide.region_1.2_spmd.sunk.clone.clone.clone.clone.sunk | while | flops 4767803 | bytes 30532288 | solution.py:160
  105.0 7.1 %collective-permute-start.3 = (f32[16,3,1,8,128]{4,3,2,0,1:T(8,128)S(1)}, f32[16,3,1,8,128]{4,3,2,0,1:T(8,128)S(1)}, u32[]{:S(2)}, u32[]{:S(2)}) collective-permute-start(f32[16,3,1,8,128]{4,3,2,0,1:T(8,128)S(1)} %pad_maximum_fusion.17), channel_id=1, source_target_pairs={{0,1},{1,2},{2,3},{3,4},{4,5},{5,6},{6,7},{8,9},{9,10},{10,11},{11... | collective-permute-start | bytes 589832 | tf_op jit(solution)/shard_map/while/body/eval_jaxpr/ppermute | solution.py:21
  119.9 7.7 %collective-permute-start.1 = (f32[16,3,1,8,128]{4,3,2,0,1:T(8,128)S(1)}, f32[16,3,1,8,128]{4,3,2,0,1:T(8,128)S(1)}, u32[]{:S(2)}, u32[]{:S(2)}) collective-permute-start(f32[16,3,1,8,128]{4,3,2,0,1:T(8,128)S(1)} %pad_maximum_fusion.16), channel_id=1, source_target_pairs={{0,1},{1,2},{2,3},{3,4},{4,5},{5,6},{6,7},{8,9},{9,10},{10,11},{11... | collective-permute-start | bytes 589832 | tf_op jit(solution)/shard_map/while/body/eval_jaxpr/ppermute | solution.py:21
  133.9 7.7 %collective-permute-start.3 = (f32[16,3,1,8,128]{4,3,2,0,1:T(8,128)S(1)}, f32[16,3,1,8,128]{4,3,2,0,1:T(8,128)S(1)}, u32[]{:S(2)}, u32[]{:S(2)}) collective-permute-start(f32[16,3,1,8,128]{4,3,2,0,1:T(8,128)S(1)} %pad_maximum_fusion.17), channel_id=1, source_target_pairs={{0,1},{1,2},{2,3},{3,4},{4,5},{5,6},{6,7},{8,9},{9,10},{10,11},{11... | collective-permute-start | bytes 589832 | tf_op jit(solution)/shard_map/while/body/eval_jaxpr/ppermute | solution.py:21
  149.4 7.7 %collective-permute-start.1 = (f32[16,3,1,8,128]{4,3,2,0,1:T(8,128)S(1)}, f32[16,3,1,8,128]{4,3,2,0,1:T(8,128)S(1)}, u32[]{:S(2)}, u32[]{:S(2)}) collective-permute-start(f32[16,3,1,8,128]{4,3,2,0,1:T(8,128)S(1)} %pad_maximum_fusion.16), channel_id=1, source_target_pairs={{0,1},{1,2},{2,3},{3,4},{4,5},{5,6},{6,7},{8,9},{9,10},{10,11},{11... | collective-permute-start | bytes 589832 | tf_op jit(solution)/shard_map/while/body/eval_jaxpr/ppermute | solution.py:21
  163.4 7.7 %collective-permute-start.3 = (f32[16,3,1,8,128]{4,3,2,0,1:T(8,128)S(1)}, f32[16,3,1,8,128]{4,3,2,0,1:T(8,128)S(1)}, u32[]{:S(2)}, u32[]{:S(2)}) collective-permute-start(f32[16,3,1,8,128]{4,3,2,0,1:T(8,128)S(1)} %pad_maximum_fusion.17), channel_id=1, source_target_pairs={{0,1},{1,2},{2,3},{3,4},{4,5},{5,6},{6,7},{8,9},{9,10},{10,11},{11... | collective-permute-start | bytes 589832 | tf_op jit(solution)/shard_map/while/body/eval_jaxpr/ppermute | solution.py:21
  179.0 7.7 %collective-permute-start.1 = (f32[16,3,1,8,128]{4,3,2,0,1:T(8,128)S(1)}, f32[16,3,1,8,128]{4,3,2,0,1:T(8,128)S(1)}, u32[]{:S(2)}, u32[]{:S(2)}) collective-permute-start(f32[16,3,1,8,128]{4,3,2,0,1:T(8,128)S(1)} %pad_maximum_fusion.16), channel_id=1, source_target_pairs={{0,1},{1,2},{2,3},{3,4},{4,5},{5,6},{6,7},{8,9},{9,10},{10,11},{11... | collective-permute-start | bytes 589832 | tf_op jit(solution)/shard_map/while/body/eval_jaxpr/ppermute | solution.py:21
  193.0 7.7 %collective-permute-start.3 = (f32[16,3,1,8,128]{4,3,2,0,1:T(8,128)S(1)}, f32[16,3,1,8,128]{4,3,2,0,1:T(8,128)S(1)}, u32[]{:S(2)}, u32[]{:S(2)}) collective-permute-start(f32[16,3,1,8,128]{4,3,2,0,1:T(8,128)S(1)} %pad_maximum_fusion.17), channel_id=1, source_target_pairs={{0,1},{1,2},{2,3},{3,4},{4,5},{5,6},{6,7},{8,9},{9,10},{10,11},{11... | collective-permute-start | bytes 589832 | tf_op jit(solution)/shard_map/while/body/eval_jaxpr/ppermute | solution.py:21
  208.5 7.7 %collective-permute-start.1 = (f32[16,3,1,8,128]{4,3,2,0,1:T(8,128)S(1)}, f32[16,3,1,8,128]{4,3,2,0,1:T(8,128)S(1)}, u32[]{:S(2)}, u32[]{:S(2)}) collective-permute-start(f32[16,3,1,8,128]{4,3,2,0,1:T(8,128)S(1)} %pad_maximum_fusion.16), channel_id=1, source_target_pairs={{0,1},{1,2},{2,3},{3,4},{4,5},{5,6},{6,7},{8,9},{9,10},{10,11},{11... | collective-permute-start | bytes 589832 | tf_op jit(solution)/shard_map/while/body/eval_jaxpr/ppermute | solution.py:21
  222.5 7.7 %collective-permute-start.3 = (f32[16,3,1,8,128]{4,3,2,0,1:T(8,128)S(1)}, f32[16,3,1,8,128]{4,3,2,0,1:T(8,128)S(1)}, u32[]{:S(2)}, u32[]{:S(2)}) collective-permute-start(f32[16,3,1,8,128]{4,3,2,0,1:T(8,128)S(1)} %pad_maximum_fusion.17), channel_id=1, source_target_pairs={{0,1},{1,2},{2,3},{3,4},{4,5},{5,6},{6,7},{8,9},{9,10},{10,11},{11... | collective-permute-start | bytes 589832 | tf_op jit(solution)/shard_map/while/body/eval_jaxpr/ppermute | solution.py:21
  238.1 7.7 %collective-permute-start.1 = (f32[16,3,1,8,128]{4,3,2,0,1:T(8,128)S(1)}, f32[16,3,1,8,128]{4,3,2,0,1:T(8,128)S(1)}, u32[]{:S(2)}, u32[]{:S(2)}) collective-permute-start(f32[16,3,1,8,128]{4,3,2,0,1:T(8,128)S(1)} %pad_maximum_fusion.16), channel_id=1, source_target_pairs={{0,1},{1,2},{2,3},{3,4},{4,5},{5,6},{6,7},{8,9},{9,10},{10,11},{11... | collective-permute-start | bytes 589832 | tf_op jit(solution)/shard_map/while/body/eval_jaxpr/ppermute | solution.py:21
  252.1 7.7 %collective-permute-start.3 = (f32[16,3,1,8,128]{4,3,2,0,1:T(8,128)S(1)}, f32[16,3,1,8,128]{4,3,2,0,1:T(8,128)S(1)}, u32[]{:S(2)}, u32[]{:S(2)}) collective-permute-start(f32[16,3,1,8,128]{4,3,2,0,1:T(8,128)S(1)} %pad_maximum_fusion.17), channel_id=1, source_target_pairs={{0,1},{1,2},{2,3},{3,4},{4,5},{5,6},{6,7},{8,9},{9,10},{10,11},{11... | collective-permute-start | bytes 589832 | tf_op jit(solution)/shard_map/while/body/eval_jaxpr/ppermute | solution.py:21
  267.6 7.7 %collective-permute-start.1 = (f32[16,3,1,8,128]{4,3,2,0,1:T(8,128)S(1)}, f32[16,3,1,8,128]{4,3,2,0,1:T(8,128)S(1)}, u32[]{:S(2)}, u32[]{:S(2)}) collective-permute-start(f32[16,3,1,8,128]{4,3,2,0,1:T(8,128)S(1)} %pad_maximum_fusion.16), channel_id=1, source_target_pairs={{0,1},{1,2},{2,3},{3,4},{4,5},{5,6},{6,7},{8,9},{9,10},{10,11},{11... | collective-permute-start | bytes 589832 | tf_op jit(solution)/shard_map/while/body/eval_jaxpr/ppermute | solution.py:21
  281.6 7.7 %collective-permute-start.3 = (f32[16,3,1,8,128]{4,3,2,0,1:T(8,128)S(1)}, f32[16,3,1,8,128]{4,3,2,0,1:T(8,128)S(1)}, u32[]{:S(2)}, u32[]{:S(2)}) collective-permute-start(f32[16,3,1,8,128]{4,3,2,0,1:T(8,128)S(1)} %pad_maximum_fusion.17), channel_id=1, source_target_pairs={{0,1},{1,2},{2,3},{3,4},{4,5},{5,6},{6,7},{8,9},{9,10},{10,11},{11... | collective-permute-start | bytes 589832 | tf_op jit(solution)/shard_map/while/body/eval_jaxpr/ppermute | solution.py:21
  297.2 7.7 %collective-permute-start.1 = (f32[16,3,1,8,128]{4,3,2,0,1:T(8,128)S(1)}, f32[16,3,1,8,128]{4,3,2,0,1:T(8,128)S(1)}, u32[]{:S(2)}, u32[]{:S(2)}) collective-permute-start(f32[16,3,1,8,128]{4,3,2,0,1:T(8,128)S(1)} %pad_maximum_fusion.16), channel_id=1, source_target_pairs={{0,1},{1,2},{2,3},{3,4},{4,5},{5,6},{6,7},{8,9},{9,10},{10,11},{11... | collective-permute-start | bytes 589832 | tf_op jit(solution)/shard_map/while/body/eval_jaxpr/ppermute | solution.py:21
  311.2 7.7 %collective-permute-start.3 = (f32[16,3,1,8,128]{4,3,2,0,1:T(8,128)S(1)}, f32[16,3,1,8,128]{4,3,2,0,1:T(8,128)S(1)}, u32[]{:S(2)}, u32[]{:S(2)}) collective-permute-start(f32[16,3,1,8,128]{4,3,2,0,1:T(8,128)S(1)} %pad_maximum_fusion.17), channel_id=1, source_target_pairs={{0,1},{1,2},{2,3},{3,4},{4,5},{5,6},{6,7},{8,9},{9,10},{10,11},{11... | collective-permute-start | bytes 589832 | tf_op jit(solution)/shard_map/while/body/eval_jaxpr/ppermute | solution.py:21
  326.7 7.7 %collective-permute-start.1 = (f32[16,3,1,8,128]{4,3,2,0,1:T(8,128)S(1)}, f32[16,3,1,8,128]{4,3,2,0,1:T(8,128)S(1)}, u32[]{:S(2)}, u32[]{:S(2)}) collective-permute-start(f32[16,3,1,8,128]{4,3,2,0,1:T(8,128)S(1)} %pad_maximum_fusion.16), channel_id=1, source_target_pairs={{0,1},{1,2},{2,3},{3,4},{4,5},{5,6},{6,7},{8,9},{9,10},{10,11},{11... | collective-permute-start | bytes 589832 | tf_op jit(solution)/shard_map/while/body/eval_jaxpr/ppermute | solution.py:21
  340.7 7.7 %collective-permute-start.3 = (f32[16,3,1,8,128]{4,3,2,0,1:T(8,128)S(1)}, f32[16,3,1,8,128]{4,3,2,0,1:T(8,128)S(1)}, u32[]{:S(2)}, u32[]{:S(2)}) collective-permute-start(f32[16,3,1,8,128]{4,3,2,0,1:T(8,128)S(1)} %pad_maximum_fusion.17), channel_id=1, source_target_pairs={{0,1},{1,2},{2,3},{3,4},{4,5},{5,6},{6,7},{8,9},{9,10},{10,11},{11... | collective-permute-start | bytes 589832 | tf_op jit(solution)/shard_map/while/body/eval_jaxpr/ppermute | solution.py:21
  356.2 7.7 %collective-permute-start.1 = (f32[16,3,1,8,128]{4,3,2,0,1:T(8,128)S(1)}, f32[16,3,1,8,128]{4,3,2,0,1:T(8,128)S(1)}, u32[]{:S(2)}, u32[]{:S(2)}) collective-permute-start(f32[16,3,1,8,128]{4,3,2,0,1:T(8,128)S(1)} %pad_maximum_fusion.16), channel_id=1, source_target_pairs={{0,1},{1,2},{2,3},{3,4},{4,5},{5,6},{6,7},{8,9},{9,10},{10,11},{11... | collective-permute-start | bytes 589832 | tf_op jit(solution)/shard_map/while/body/eval_jaxpr/ppermute | solution.py:21
  370.3 7.7 %collective-permute-start.3 = (f32[16,3,1,8,128]{4,3,2,0,1:T(8,128)S(1)}, f32[16,3,1,8,128]{4,3,2,0,1:T(8,128)S(1)}, u32[]{:S(2)}, u32[]{:S(2)}) collective-permute-start(f32[16,3,1,8,128]{4,3,2,0,1:T(8,128)S(1)} %pad_maximum_fusion.17), channel_id=1, source_target_pairs={{0,1},{1,2},{2,3},{3,4},{4,5},{5,6},{6,7},{8,9},{9,10},{10,11},{11... | collective-permute-start | bytes 589832 | tf_op jit(solution)/shard_map/while/body/eval_jaxpr/ppermute | solution.py:21
  385.4 12.6 %all-to-all-done.2 = f32[16,4,12,128]{3,0,2,1:T(8,128)S(1)} async-done(((f32[16,4,12,128]{3,0,2,1:T(8,128)}), f32[16,4,12,128]{3,0,2,1:T(8,128)S(1)}, u32[]{:S(2)}, u32[]{:S(2)}) %all-to-all-start.2) | async-done | bytes 393248 | tf_op jit(solution)/shard_map/all_to_all | solution.py:167
  399.1 14.8 %all_to_all.60 = f32[64,1,12,128]{3,1,2,0:T(1,128)S(1)} all-to-all(f32[64,1,12,128]{3,1,2,0:T(1,128)S(1)} %copy.94), channel_id=1, replica_groups=mesh['tm'=4,'space'=8] {'tm'}, dimensions={0} | all-to-all | bytes 786432 | tf_op jit(solution)/shard_map/all_to_all | solution.py:170
  (563 shorter events, 207.4 us)
Async XLA Ops:
  1.9 18.0 %all-to-all-start = ((f32[16,4,12,128]{3,0,2,1:T(8,128)}), f32[16,4,12,128]{3,0,2,1:T(8,128)S(1)}, u32[]{:S(2)}, u32[]{:S(2)}) async-start(f32[16,4,12,128]{3,0,2,1:T(8,128)} %bitcast.2), calls=%async_computation | async-start | bytes 786432 | tf_op jit(solution)/shard_map/all_to_all | solution.py:128
  21.7 25.7 %all-to-all-start.1 = ((f32[64,1,12,128]{3,1,2,0:T(1,128)}), f32[64,1,12,128]{3,1,2,0:T(1,128)S(1)}, u32[]{:S(2)}, u32[]{:S(2)}) async-start(f32[64,1,12,128]{3,1,2,0:T(1,128)} %copy.86), calls=%async_computation.1 | async-start | bytes 786432 | tf_op jit(solution)/shard_map/all_to_all | solution.py:131
  64.1 7.9 %collective-permute-start.1 = (f32[16,3,1,8,128]{4,3,2,0,1:T(8,128)S(1)}, f32[16,3,1,8,128]{4,3,2,0,1:T(8,128)S(1)}, u32[]{:S(2)}, u32[]{:S(2)}) collective-permute-start(f32[16,3,1,8,128]{4,3,2,0,1:T(8,128)S(1)} %pad_maximum_fusion.16), channel_id=1, source_target_pairs={{0,1},{1,2},{2,3},{3,4},{4,5},{5,6},{6,7},{8,9},{9,10},{10,11},{11... | collective-permute-start | bytes 589832 | tf_op jit(solution)/shard_map/while/body/eval_jaxpr/ppermute | solution.py:21
  77.2 7.9 %collective-permute-start.3 = (f32[16,3,1,8,128]{4,3,2,0,1:T(8,128)S(1)}, f32[16,3,1,8,128]{4,3,2,0,1:T(8,128)S(1)}, u32[]{:S(2)}, u32[]{:S(2)}) collective-permute-start(f32[16,3,1,8,128]{4,3,2,0,1:T(8,128)S(1)} %pad_maximum_fusion.17), channel_id=1, source_target_pairs={{0,1},{1,2},{2,3},{3,4},{4,5},{5,6},{6,7},{8,9},{9,10},{10,11},{11... | collective-permute-start | bytes 589832 | tf_op jit(solution)/shard_map/while/body/eval_jaxpr/ppermute | solution.py:21
  105.0 8.1 %collective-permute-start.3 = (f32[16,3,1,8,128]{4,3,2,0,1:T(8,128)S(1)}, f32[16,3,1,8,128]{4,3,2,0,1:T(8,128)S(1)}, u32[]{:S(2)}, u32[]{:S(2)}) collective-permute-start(f32[16,3,1,8,128]{4,3,2,0,1:T(8,128)S(1)} %pad_maximum_fusion.17), channel_id=1, source_target_pairs={{0,1},{1,2},{2,3},{3,4},{4,5},{5,6},{6,7},{8,9},{9,10},{10,11},{11... | collective-permute-start | bytes 589832 | tf_op jit(solution)/shard_map/while/body/eval_jaxpr/ppermute | solution.py:21
  119.9 8.8 %collective-permute-start.1 = (f32[16,3,1,8,128]{4,3,2,0,1:T(8,128)S(1)}, f32[16,3,1,8,128]{4,3,2,0,1:T(8,128)S(1)}, u32[]{:S(2)}, u32[]{:S(2)}) collective-permute-start(f32[16,3,1,8,128]{4,3,2,0,1:T(8,128)S(1)} %pad_maximum_fusion.16), channel_id=1, source_target_pairs={{0,1},{1,2},{2,3},{3,4},{4,5},{5,6},{6,7},{8,9},{9,10},{10,11},{11... | collective-permute-start | bytes 589832 | tf_op jit(solution)/shard_map/while/body/eval_jaxpr/ppermute | solution.py:21
  133.9 8.8 %collective-permute-start.3 = (f32[16,3,1,8,128]{4,3,2,0,1:T(8,128)S(1)}, f32[16,3,1,8,128]{4,3,2,0,1:T(8,128)S(1)}, u32[]{:S(2)}, u32[]{:S(2)}) collective-permute-start(f32[16,3,1,8,128]{4,3,2,0,1:T(8,128)S(1)} %pad_maximum_fusion.17), channel_id=1, source_target_pairs={{0,1},{1,2},{2,3},{3,4},{4,5},{5,6},{6,7},{8,9},{9,10},{10,11},{11... | collective-permute-start | bytes 589832 | tf_op jit(solution)/shard_map/while/body/eval_jaxpr/ppermute | solution.py:21
  149.4 8.8 %collective-permute-start.1 = (f32[16,3,1,8,128]{4,3,2,0,1:T(8,128)S(1)}, f32[16,3,1,8,128]{4,3,2,0,1:T(8,128)S(1)}, u32[]{:S(2)}, u32[]{:S(2)}) collective-permute-start(f32[16,3,1,8,128]{4,3,2,0,1:T(8,128)S(1)} %pad_maximum_fusion.16), channel_id=1, source_target_pairs={{0,1},{1,2},{2,3},{3,4},{4,5},{5,6},{6,7},{8,9},{9,10},{10,11},{11... | collective-permute-start | bytes 589832 | tf_op jit(solution)/shard_map/while/body/eval_jaxpr/ppermute | solution.py:21
  163.4 8.8 %collective-permute-start.3 = (f32[16,3,1,8,128]{4,3,2,0,1:T(8,128)S(1)}, f32[16,3,1,8,128]{4,3,2,0,1:T(8,128)S(1)}, u32[]{:S(2)}, u32[]{:S(2)}) collective-permute-start(f32[16,3,1,8,128]{4,3,2,0,1:T(8,128)S(1)} %pad_maximum_fusion.17), channel_id=1, source_target_pairs={{0,1},{1,2},{2,3},{3,4},{4,5},{5,6},{6,7},{8,9},{9,10},{10,11},{11... | collective-permute-start | bytes 589832 | tf_op jit(solution)/shard_map/while/body/eval_jaxpr/ppermute | solution.py:21
  179.0 8.8 %collective-permute-start.1 = (f32[16,3,1,8,128]{4,3,2,0,1:T(8,128)S(1)}, f32[16,3,1,8,128]{4,3,2,0,1:T(8,128)S(1)}, u32[]{:S(2)}, u32[]{:S(2)}) collective-permute-start(f32[16,3,1,8,128]{4,3,2,0,1:T(8,128)S(1)} %pad_maximum_fusion.16), channel_id=1, source_target_pairs={{0,1},{1,2},{2,3},{3,4},{4,5},{5,6},{6,7},{8,9},{9,10},{10,11},{11... | collective-permute-start | bytes 589832 | tf_op jit(solution)/shard_map/while/body/eval_jaxpr/ppermute | solution.py:21
  193.0 8.8 %collective-permute-start.3 = (f32[16,3,1,8,128]{4,3,2,0,1:T(8,128)S(1)}, f32[16,3,1,8,128]{4,3,2,0,1:T(8,128)S(1)}, u32[]{:S(2)}, u32[]{:S(2)}) collective-permute-start(f32[16,3,1,8,128]{4,3,2,0,1:T(8,128)S(1)} %pad_maximum_fusion.17), channel_id=1, source_target_pairs={{0,1},{1,2},{2,3},{3,4},{4,5},{5,6},{6,7},{8,9},{9,10},{10,11},{11... | collective-permute-start | bytes 589832 | tf_op jit(solution)/shard_map/while/body/eval_jaxpr/ppermute | solution.py:21
  208.5 8.8 %collective-permute-start.1 = (f32[16,3,1,8,128]{4,3,2,0,1:T(8,128)S(1)}, f32[16,3,1,8,128]{4,3,2,0,1:T(8,128)S(1)}, u32[]{:S(2)}, u32[]{:S(2)}) collective-permute-start(f32[16,3,1,8,128]{4,3,2,0,1:T(8,128)S(1)} %pad_maximum_fusion.16), channel_id=1, source_target_pairs={{0,1},{1,2},{2,3},{3,4},{4,5},{5,6},{6,7},{8,9},{9,10},{10,11},{11... | collective-permute-start | bytes 589832 | tf_op jit(solution)/shard_map/while/body/eval_jaxpr/ppermute | solution.py:21
  222.5 8.8 %collective-permute-start.3 = (f32[16,3,1,8,128]{4,3,2,0,1:T(8,128)S(1)}, f32[16,3,1,8,128]{4,3,2,0,1:T(8,128)S(1)}, u32[]{:S(2)}, u32[]{:S(2)}) collective-permute-start(f32[16,3,1,8,128]{4,3,2,0,1:T(8,128)S(1)} %pad_maximum_fusion.17), channel_id=1, source_target_pairs={{0,1},{1,2},{2,3},{3,4},{4,5},{5,6},{6,7},{8,9},{9,10},{10,11},{11... | collective-permute-start | bytes 589832 | tf_op jit(solution)/shard_map/while/body/eval_jaxpr/ppermute | solution.py:21
  238.1 8.8 %collective-permute-start.1 = (f32[16,3,1,8,128]{4,3,2,0,1:T(8,128)S(1)}, f32[16,3,1,8,128]{4,3,2,0,1:T(8,128)S(1)}, u32[]{:S(2)}, u32[]{:S(2)}) collective-permute-start(f32[16,3,1,8,128]{4,3,2,0,1:T(8,128)S(1)} %pad_maximum_fusion.16), channel_id=1, source_target_pairs={{0,1},{1,2},{2,3},{3,4},{4,5},{5,6},{6,7},{8,9},{9,10},{10,11},{11... | collective-permute-start | bytes 589832 | tf_op jit(solution)/shard_map/while/body/eval_jaxpr/ppermute | solution.py:21
  252.1 8.8 %collective-permute-start.3 = (f32[16,3,1,8,128]{4,3,2,0,1:T(8,128)S(1)}, f32[16,3,1,8,128]{4,3,2,0,1:T(8,128)S(1)}, u32[]{:S(2)}, u32[]{:S(2)}) collective-permute-start(f32[16,3,1,8,128]{4,3,2,0,1:T(8,128)S(1)} %pad_maximum_fusion.17), channel_id=1, source_target_pairs={{0,1},{1,2},{2,3},{3,4},{4,5},{5,6},{6,7},{8,9},{9,10},{10,11},{11... | collective-permute-start | bytes 589832 | tf_op jit(solution)/shard_map/while/body/eval_jaxpr/ppermute | solution.py:21
  267.6 8.8 %collective-permute-start.1 = (f32[16,3,1,8,128]{4,3,2,0,1:T(8,128)S(1)}, f32[16,3,1,8,128]{4,3,2,0,1:T(8,128)S(1)}, u32[]{:S(2)}, u32[]{:S(2)}) collective-permute-start(f32[16,3,1,8,128]{4,3,2,0,1:T(8,128)S(1)} %pad_maximum_fusion.16), channel_id=1, source_target_pairs={{0,1},{1,2},{2,3},{3,4},{4,5},{5,6},{6,7},{8,9},{9,10},{10,11},{11... | collective-permute-start | bytes 589832 | tf_op jit(solution)/shard_map/while/body/eval_jaxpr/ppermute | solution.py:21
  281.6 8.8 %collective-permute-start.3 = (f32[16,3,1,8,128]{4,3,2,0,1:T(8,128)S(1)}, f32[16,3,1,8,128]{4,3,2,0,1:T(8,128)S(1)}, u32[]{:S(2)}, u32[]{:S(2)}) collective-permute-start(f32[16,3,1,8,128]{4,3,2,0,1:T(8,128)S(1)} %pad_maximum_fusion.17), channel_id=1, source_target_pairs={{0,1},{1,2},{2,3},{3,4},{4,5},{5,6},{6,7},{8,9},{9,10},{10,11},{11... | collective-permute-start | bytes 589832 | tf_op jit(solution)/shard_map/while/body/eval_jaxpr/ppermute | solution.py:21
  297.2 8.8 %collective-permute-start.1 = (f32[16,3,1,8,128]{4,3,2,0,1:T(8,128)S(1)}, f32[16,3,1,8,128]{4,3,2,0,1:T(8,128)S(1)}, u32[]{:S(2)}, u32[]{:S(2)}) collective-permute-start(f32[16,3,1,8,128]{4,3,2,0,1:T(8,128)S(1)} %pad_maximum_fusion.16), channel_id=1, source_target_pairs={{0,1},{1,2},{2,3},{3,4},{4,5},{5,6},{6,7},{8,9},{9,10},{10,11},{11... | collective-permute-start | bytes 589832 | tf_op jit(solution)/shard_map/while/body/eval_jaxpr/ppermute | solution.py:21
  311.2 8.8 %collective-permute-start.3 = (f32[16,3,1,8,128]{4,3,2,0,1:T(8,128)S(1)}, f32[16,3,1,8,128]{4,3,2,0,1:T(8,128)S(1)}, u32[]{:S(2)}, u32[]{:S(2)}) collective-permute-start(f32[16,3,1,8,128]{4,3,2,0,1:T(8,128)S(1)} %pad_maximum_fusion.17), channel_id=1, source_target_pairs={{0,1},{1,2},{2,3},{3,4},{4,5},{5,6},{6,7},{8,9},{9,10},{10,11},{11... | collective-permute-start | bytes 589832 | tf_op jit(solution)/shard_map/while/body/eval_jaxpr/ppermute | solution.py:21
  326.7 8.8 %collective-permute-start.1 = (f32[16,3,1,8,128]{4,3,2,0,1:T(8,128)S(1)}, f32[16,3,1,8,128]{4,3,2,0,1:T(8,128)S(1)}, u32[]{:S(2)}, u32[]{:S(2)}) collective-permute-start(f32[16,3,1,8,128]{4,3,2,0,1:T(8,128)S(1)} %pad_maximum_fusion.16), channel_id=1, source_target_pairs={{0,1},{1,2},{2,3},{3,4},{4,5},{5,6},{6,7},{8,9},{9,10},{10,11},{11... | collective-permute-start | bytes 589832 | tf_op jit(solution)/shard_map/while/body/eval_jaxpr/ppermute | solution.py:21
  340.7 8.8 %collective-permute-start.3 = (f32[16,3,1,8,128]{4,3,2,0,1:T(8,128)S(1)}, f32[16,3,1,8,128]{4,3,2,0,1:T(8,128)S(1)}, u32[]{:S(2)}, u32[]{:S(2)}) collective-permute-start(f32[16,3,1,8,128]{4,3,2,0,1:T(8,128)S(1)} %pad_maximum_fusion.17), channel_id=1, source_target_pairs={{0,1},{1,2},{2,3},{3,4},{4,5},{5,6},{6,7},{8,9},{9,10},{10,11},{11... | collective-permute-start | bytes 589832 | tf_op jit(solution)/shard_map/while/body/eval_jaxpr/ppermute | solution.py:21
  356.2 8.8 %collective-permute-start.1 = (f32[16,3,1,8,128]{4,3,2,0,1:T(8,128)S(1)}, f32[16,3,1,8,128]{4,3,2,0,1:T(8,128)S(1)}, u32[]{:S(2)}, u32[]{:S(2)}) collective-permute-start(f32[16,3,1,8,128]{4,3,2,0,1:T(8,128)S(1)} %pad_maximum_fusion.16), channel_id=1, source_target_pairs={{0,1},{1,2},{2,3},{3,4},{4,5},{5,6},{6,7},{8,9},{9,10},{10,11},{11... | collective-permute-start | bytes 589832 | tf_op jit(solution)/shard_map/while/body/eval_jaxpr/ppermute | solution.py:21
  370.3 8.8 %collective-permute-start.3 = (f32[16,3,1,8,128]{4,3,2,0,1:T(8,128)S(1)}, f32[16,3,1,8,128]{4,3,2,0,1:T(8,128)S(1)}, u32[]{:S(2)}, u32[]{:S(2)}) collective-permute-start(f32[16,3,1,8,128]{4,3,2,0,1:T(8,128)S(1)} %pad_maximum_fusion.17), channel_id=1, source_target_pairs={{0,1},{1,2},{2,3},{3,4},{4,5},{5,6},{6,7},{8,9},{9,10},{10,11},{11... | collective-permute-start | bytes 589832 | tf_op jit(solution)/shard_map/while/body/eval_jaxpr/ppermute | solution.py:21
  381.9 16.1 %all-to-all-start.2 = ((f32[16,4,12,128]{3,0,2,1:T(8,128)}), f32[16,4,12,128]{3,0,2,1:T(8,128)S(1)}, u32[]{:S(2)}, u32[]{:S(2)}) async-start(f32[16,4,12,128]{3,0,2,1:T(8,128)} %bitcast.28), calls=%async_computation.2 | async-start | bytes 786432 | tf_op jit(solution)/shard_map/all_to_all | solution.py:167
  (30 other events, 158.1 us)
where the time goes:
time: 419 us; the launch traced here: 415 us
  starting transfers between devices  215 us (51%)
  waiting for transfers between devices  101 us (24%)
  blocking collectives  34.4 us (8%)
  other arithmetic  31.9 us (8%)
  local copies, waits for them, and re-layouts  27.8 us (7%)
    ppermute x46, starting transfers between devices, from_behind(): lax.ppermute(value, axis, [(source, source + steps) for source in range(i...  202 us
    ppermute x46, waiting for transfers between devices, from_behind(): lax.ppermute(value, axis, [(source, source + steps) for source in range(i...  77.5 us
    psum x1, blocking collectives, broadcast(): return lax.psum(jnp.where(mine, array, jnp.zeros_like(array)), axis)  19.6 us
    add x11, other arithmetic, sweep(): carry_terms[sweep_index] * direction + push_terms[sweep_index] * residual  17 us
    all_to_all x1, blocking collectives, per_device(): lax.all_to_all(spread_back, 'tm', split_axis=0, concat_axis=1, tiled=True)  14.8 us
    all_to_all x1, waiting for transfers between devices, per_device(): lax.all_to_all(solution, 'tm', split_axis=1, concat_axis=0, tiled=True)  12.6 us
    all_to_all x1, waiting for transfers between devices, per_device(): lax.all_to_all(flat, 'tm', split_axis=1, concat_axis=0, tiled=True)  10.8 us
  transfers between devices with their start and end apart: 49, of which 48 were waited for; matrix products, arithmetic and copies ran while one was open for 5% of the time, Pallas kernels for 0%

commit v1 on v0

--- a/solution.py
+++ b/solution.py
@@ -1,8 +1,13 @@
 import math
+
+import functools
 
 import jax
 import jax.numpy as jnp
+import numpy as np
 from jax import lax
+from jax.experimental import pallas as pl
+from jax.experimental.pallas import tpu as pltpu
 from jax.sharding import PartitionSpec as P
 
 SWEEPS = 12
@@ -171,6 +176,335 @@
     return updated.reshape(forcing.shape)
 
 
+CHUNKS = 6
+
+
+def pair_numbers(window, groups, spots):
+    table = np.zeros((groups, spots), np.int64)
+    for z in range(groups):
+        for s in range(spots):
+            table[z, s] = 2 * (spots * (z % 2) + s) + z // 2
+    return table
+
+
+def host_tables(window, groups, spots):
+    steps = window // groups
+    gamma = ALPHA ** (1.0 / window)
+    pairs = pair_numbers(window, groups, spots)
+    cas = lambda k, n: np.cos(2 * np.pi * ((k * n) % window) / window) + np.sin(
+        2 * np.pi * ((k * n) % window) / window
+    )
+    rows = np.arange(steps)
+    merge = np.zeros((groups, 2, steps))
+    split = np.zeros((groups, 2, steps))
+    ahead = np.zeros((groups, spots, 2, 2, steps))
+    back = np.zeros((groups, 2, steps, spots, 2))
+    last = np.zeros((groups, 2))
+    for z in range(groups):
+        mine, other = steps * z + rows, steps * ((z + 2) % 4) + rows
+        upper = z // 2
+        merge[z, 0] = (-1.0 if upper else 1.0) * gamma**mine
+        merge[z, 1] = gamma**other
+        split[z, 0] = (-1.0 if upper else 1.0) * gamma**-mine / window
+        split[z, 1] = gamma**-mine / window
+        for s in range(spots):
+            j = pairs[z, s]
+            for f, k in enumerate((j, window // 2 if j == 0 else window - j)):
+                for side, low in enumerate((z % 2, 1 - z % 2)):
+                    ahead[z, s, f, side] = cas(k, steps * low + rows)
+                    back[z, side, :, s, f] = cas(k, steps * low + rows)
+    last[1, 1] = 1.0
+    last[3, 0] = 1.0
+    theta = 2 * np.pi * pairs / window
+    plain = 1 - gamma * np.cos(theta)
+    p_plus = np.where(pairs == 0, 1 - gamma, plain)
+    p_minus = np.where(pairs == 0, 1 + gamma, plain)
+    cross = np.where(pairs == 0, 0.0, gamma * np.sin(theta))
+    scale = (np.sqrt(np.maximum(p_plus, p_minus) ** 2 + cross**2) * SIGMA_TOP + CURL_TOP) ** 2
+    coef = np.stack([p_plus, p_minus, cross, 1 / scale], -1)
+    center, radius = (UPPER + LOWER) / 2, (UPPER - LOWER) / 2
+    now, cheb = radius / center, []
+    for _ in range(SWEEPS - 1):
+        later = 1.0 / (2.0 * center / radius - now)
+        cheb += [later * now, 2.0 * later / radius]
+        now = later
+    flat = lambda value: np.asarray(value, np.float32).reshape(-1)
+    return [flat(v) for v in (merge, ahead, last, coef, cheb, back, split)], 1 / center
+
+
+def window_kernel(
+    steps, spots, inverse_center,
+    merge, ahead, last, coef, cheb, back, split, conductance,
+    force, start, region, iterate, out,
+    got_last, got_far, mixed, got_near, extra, got_extra, mine_freq, spec, sigma,
+    first, res, step, total, home, half, got_half, even, got_even,
+    last_sem, far_sem, near_sem, extra_sem, sigma_sem, spec_sem, home_sem, half_sem, even_sem,
+):
+    z, s = lax.axis_index("tm"), lax.axis_index("space")
+    far = ((z + 2) % 4, s)
+    near = (z + 1 - 2 * (z % 2), s)
+    peers = [(z, (s + hop) % spots) for hop in range(1, spots)]
+    width = 6 // CHUNKS
+    planes = 2 * spots
+    parts = [pl.ds(c * width, width) for c in range(CHUNKS)]
+    sent = []
+
+    def send(source, target, sems, slot, device):
+        copy = pltpu.make_async_remote_copy(
+            src_ref=source, dst_ref=target,
+            send_sem=sems.at[(0,) + slot], recv_sem=sems.at[(1,) + slot],
+            device_id=device, device_id_type=pl.DeviceIdType.MESH,
+        )
+        copy.start()
+        sent.append(copy)
+        return copy
+
+    barrier = pltpu.get_barrier_semaphore()
+    for device in [far, near] + peers:
+        pl.semaphore_signal(barrier, inc=1, device_id=device, device_id_type=pl.DeviceIdType.MESH)
+
+    material = region[...]
+    brick_sigma = jnp.zeros(material.shape, jnp.float32)
+    for index in range(3):
+        brick_sigma = brick_sigma + jnp.where(material == index, conductance[index], 0.0)
+    sigma[s] = brick_sigma
+    pl.semaphore_wait(barrier, 2 + len(peers))
+
+    last_copy = send(iterate.at[steps - 1], got_last, last_sem, (0,), far)
+    far_copies = [
+        send(force.at[:, part], got_far.at[:, part], far_sem, (c,), far)
+        for c, part in enumerate(parts)
+    ]
+    sigma_copies = [
+        send(sigma.at[s], sigma.at[s], sigma_sem, (h,), peer) for h, peer in enumerate(peers)
+    ]
+    last_copy.wait_recv()
+    extra[...] = last[z * 2] * iterate[steps - 1] + last[z * 2 + 1] * got_last[...]
+    extra_copy = send(extra, got_extra, extra_sem, (0,), near)
+
+    def mix(c):
+        far_copies[c].wait_recv()
+
+        def row(m, carry):
+            w_mine, w_other = merge[z * 2 * steps + m], merge[(z * 2 + 1) * steps + m]
+            for t in range(c * width, (c + 1) * width):
+                mixed[m, t] = w_mine * force[m, t] + w_other * got_far[m, t]
+            return carry
+
+        lax.fori_loop(0, steps, row, 0, unroll=4)
+        return send(mixed.at[:, parts[c]], got_near.at[:, parts[c]], near_sem, (c,), near)
+
+    spec_copies = [None] * CHUNKS
+
+    def transform(c, copy):
+        copy.wait_recv()
+        if c == 0:
+            extra_copy.wait_recv()
+            got_extra[...] = start[...] - ALPHA * (extra[...] + got_extra[...])
+        jump = [brick_sigma[t % 2] * got_extra[t] for t in range(c * width, (c + 1) * width)]
+
+        def slot(k, carry):
+            base = (z * 2 * spots + k) * 2 * steps
+            sums = [[j, None] for j in jump]
+            for m in range(steps):
+                w_mine, w_other = ahead[base + m], ahead[base + steps + m]
+                for i in range(width):
+                    t = c * width + i
+                    term = w_other * got_near[m, t]
+                    sums[i][0] = sums[i][0] + w_mine * mixed[m, t]
+                    sums[i][1] = term if m == 0 else sums[i][1] + term
+            for i in range(width):
+                mine_freq[k // 2, c * width + i, k % 2] = sums[i][0] + sums[i][1]
+            return carry
+
+        lax.fori_loop(0, 2 * spots, slot, 0)
+        spec[s, parts[c]] = mine_freq[s, parts[c]]
+        spec_copies[c] = [
+            send(mine_freq.at[peer[1], parts[c]], spec.at[s, parts[c]], spec_sem, (c, h), peer)
+            for h, peer in enumerate(peers)
+        ]
+
+    pending = mix(0)
+    for c in range(CHUNKS):
+        later = mix(c + 1) if c + 1 < CHUNKS else None
+        transform(c, pending)
+        pending = later
+    for copy in sigma_copies + [copy for group in spec_copies for copy in group]:
+        copy.wait_recv()
+
+    device = z * spots + s
+    p_plus, p_minus = coef[device * 4], coef[device * 4 + 1]
+    cross, inverse_scale = coef[device * 4 + 2], coef[device * 4 + 3]
+    along_y = lax.broadcasted_iota(jnp.int32, (8, 128), 0)
+    along_z = lax.broadcasted_iota(jnp.int32, (8, 128), 1)
+    not_top_y, not_top_z = along_y < 7, along_z < 127
+    not_low_y, not_low_z = along_y > 0, along_z > 0
+    zero = jnp.zeros((8, 128), jnp.float32)
+
+    def up_y(v):
+        return jnp.where(not_top_y, pltpu.roll(v, 7, 0), 0.0)
+
+    def up_z(v):
+        return jnp.where(not_top_z, pltpu.roll(v, 127, 1), 0.0)
+
+    def down_y(v):
+        return jnp.where(not_low_y, pltpu.roll(v, 1, 0), 0.0)
+
+    def down_z(v):
+        return jnp.where(not_low_z, pltpu.roll(v, 1, 1), 0.0)
+
+    def operator(buffer, sign, finish):
+        load = lambda i: [[buffer[i // 2, 2 * e + i % 2, f] for e in range(3)] for f in range(2)]
+        here = load(0)
+        behind = [(zero, zero), (zero, zero)]
+        for i in range(planes):
+            ahead_field = load(i + 1) if i + 1 < planes else [[zero] * 3] * 2
+            weight = sigma[i // 2, i % 2]
+            weights = (weight * p_plus, weight * p_minus)
+            weight_cross = weight * cross
+            for f in range(2):
+                ex, ey, ez = here[f]
+                _, ey1, ez1 = ahead_field[f]
+                bx = (up_y(ez) - ez) - (up_z(ey) - ey)
+                by = (up_z(ex) - ex) - (ez1 - ez)
+                bz = (ey1 - ey) - (up_y(ex) - ex)
+                by0, bz0 = behind[f]
+                curls = (
+                    (down_z(by) - by) - (down_y(bz) - bz),
+                    (bz0 - bz) - (down_z(bx) - bx),
+                    (down_y(bx) - bx) - (by0 - by),
+                )
+                behind[f] = (by, bz)
+                for e in range(3):
+                    own = weights[f] * here[f][e]
+                    swapped = weight_cross * here[1 - f][e]
+                    value = curls[e] + own
+                    value = value + swapped if (f == 1) == (sign > 0) else value - swapped
+                    finish(i, e, f, value)
+            here = ahead_field
+
+    def begin(i, e, f, value):
+        at = (i // 2, 2 * e + i % 2, f)
+        g = value * inverse_scale
+        res[at] = g
+        step[at] = g * inverse_center
+        total[at] = zero
+
+    operator(spec, -1.0, begin)
+
+    def sweep(index, carry):
+        w_step, w_res = cheb[index * 2], cheb[index * 2 + 1]
+
+        def keep(i, e, f, value):
+            first[i // 2, 2 * e + i % 2, f] = value
+
+        def advance(i, e, f, value):
+            at = (i // 2, 2 * e + i % 2, f)
+            old = step[at]
+            total[at] = total[at] + old
+            new = res[at] - value * inverse_scale
+            res[at] = new
+            step[at] = w_step * old + w_res * new
+
+        operator(step, 1.0, keep)
+        operator(first, -1.0, advance)
+        return carry
+
+    lax.fori_loop(0, SWEEPS - 1, sweep, 0)
+
+    home_copies = []
+    for c, part in enumerate(parts):
+        for b in range(spots):
+            for t in range(c * width, (c + 1) * width):
+                for f in range(2):
+                    total[b, t, f] = total[b, t, f] + step[b, t, f]
+        home[s, part] = total[s, part]
+        home_copies.append([
+            send(total.at[peer[1], part], home.at[s, part], home_sem, (c, h), peer)
+            for h, peer in enumerate(peers)
+        ])
+
+    def gather(c):
+        for copy in home_copies[c]:
+            copy.wait_recv()
+
+        def row(m, carry):
+            base_mine = (z * 2 * steps + m) * 2 * spots
+            base_other = ((z * 2 + 1) * steps + m) * 2 * spots
+            for t in range(c * width, (c + 1) * width):
+                mine, other = None, None
+                for b in range(spots):
+                    for f in range(2):
+                        value = home[b, t, f]
+                        term = back[base_mine + 2 * b + f] * value
+                        mine = term if mine is None else mine + term
+                        term = back[base_other + 2 * b + f] * value
+                        other = term if other is None else other + term
+                even[m, t] = mine
+                half[m, t] = other
+            return carry
+
+        lax.fori_loop(0, steps, row, 0)
+        return send(half.at[:, parts[c]], got_half.at[:, parts[c]], half_sem, (c,), near)
+
+    def add(c, copy):
+        copy.wait_recv()
+        even[:, parts[c]] = even[:, parts[c]] + got_half[:, parts[c]]
+        return send(even.at[:, parts[c]], got_even.at[:, parts[c]], even_sem, (c,), far)
+
+    half_copies = [gather(0)]
+    even_copies = []
+    for c in range(CHUNKS):
+        if c + 1 < CHUNKS:
+            half_copies.append(gather(c + 1))
+        even_copies.append(add(c, half_copies[c]))
+    for c in range(CHUNKS):
+        even_copies[c].wait_recv()
+
+        def row(m, carry):
+            w_mine, w_other = split[z * 2 * steps + m], split[(z * 2 + 1) * steps + m]
+            for t in range(c * width, (c + 1) * width):
+                out[m, t] = w_mine * even[m, t] + w_other * got_even[m, t]
+            return carry
+
+        lax.fori_loop(0, steps, row, 0, unroll=4)
+    for copy in sent:
+        copy.wait_send()
+
+
+def pair_per_device(groups, spots, forcing, start_field, iterate, region, conductance):
+    steps = forcing.shape[0]
+    tables, inverse_center = host_tables(steps * groups, groups, spots)
+    tile = forcing.shape[3:]
+    f32 = jnp.float32
+    brick = lambda *lead: pltpu.VMEM(lead + tile, f32)
+    rows = brick(steps, 6)
+    grid = brick(spots, 6, 2)
+    dma = pltpu.SemaphoreType.DMA
+    smem, vmem = pl.BlockSpec(memory_space=pltpu.SMEM), pl.BlockSpec(memory_space=pltpu.VMEM)
+    result = pl.pallas_call(
+        functools.partial(window_kernel, steps, spots, inverse_center),
+        out_shape=jax.ShapeDtypeStruct((steps, 6) + tile, f32),
+        in_specs=[smem] * 8 + [vmem] * 4,
+        out_specs=vmem,
+        scratch_shapes=[
+            brick(6), rows, rows, rows, brick(6), brick(6), grid, grid, brick(spots, 2),
+            grid, grid, grid, grid, grid, rows, rows, rows, rows,
+            dma((2, 1)), dma((2, CHUNKS)), dma((2, CHUNKS)), dma((2, 1)), dma((2, spots - 1)),
+            dma((2, CHUNKS, spots - 1)), dma((2, CHUNKS, spots - 1)),
+            dma((2, CHUNKS)), dma((2, CHUNKS)),
+        ],
+        compiler_params=pltpu.CompilerParams(
+            collective_id=0, has_side_effects=True, vmem_limit_bytes=32 * 1024 * 1024
+        ),
+    )(
+        *[jnp.asarray(table) for table in tables], conductance,
+        forcing.reshape((steps, 6) + tile), start_field.reshape((6,) + tile), region,
+        iterate.reshape((steps, 6) + tile),
+    )
+    return result.reshape(forcing.shape)
+
+
 def solution(mesh):
     placed = (
         P("tm", None, "space", None, None),
@@ -179,8 +513,17 @@
         P("space", None, None),
         P(),
     )
+    groups, spots = mesh.shape["tm"], mesh.shape["space"]
+
+    def per_block(*arrays):
+        steps, planes = arrays[0].shape[0], arrays[0].shape[2]
+        one_each = steps * groups == 2 * groups * spots
+        if groups == 4 and one_each and planes == 2 and arrays[0].shape[3:] == (8, 128):
+            return pair_per_device(groups, spots, *arrays)
+        return per_device(*arrays)
+
     return jax.shard_map(
-        per_device,
+        per_block,
         mesh=mesh,
         in_specs=placed,
         out_specs=P("tm", None, "space", None, None),

time: 419 us -> 83.6 us (0.20)
  starting transfers between devices: 215 us -> 0 us
  waiting for transfers between devices: 101 us -> 0 us
  Pallas kernels: 0 us -> 77.6 us
  blocking collectives: 34.4 us -> 0 us
  other arithmetic: 31.9 us -> 0 us
  local copies, waits for them, and re-layouts: 27.8 us -> 5.59 us
    ppermute x46 -> x0, starting transfers between devices: 202 us -> none  [from_behind(): lax.ppermute(value, axis, [(source, source + steps) for source in range(i...]
    pallas_call x0 -> x1, Pallas kernels: none -> 77.6 us  [pair_per_device(): pl.pallas_call(functools.partial(window_kernel, steps, spots, inverse_cen...]
    ppermute x46 -> x0, waiting for transfers between devices: 77.5 us -> none  [from_behind(): lax.ppermute(value, axis, [(source, source + steps) for source in range(i...]
    all_to_all x3 -> x0, waiting for transfers between devices: 23.4 us -> none  [the longest x1 12.6 us: per_device(): lax.all_to_all(solution, 'tm', split_axis=1, concat_axis=0, tiled=True)]
    add x25 -> x0, other arithmetic: 21.3 us -> none  [the longest x11 17 us: sweep(): carry_terms[sweep_index] * direction + push_terms[sweep_index] * residual]
    psum x1 -> x0, blocking collectives: 19.6 us -> none  [broadcast(): return lax.psum(jnp.where(mine, array, jnp.zeros_like(array)), axis)]
    all_to_all x1 -> x0, blocking collectives: 14.8 us -> none  [per_device(): lax.all_to_all(spread_back, 'tm', split_axis=0, concat_axis=1, tiled=True)]
    dynamic_slice x22 -> x0, local copies, waits for them, and re-layouts: 13.5 us -> none  [the longest x11 7 us: sweep(): carry_terms[sweep_index] * direction + push_terms[sweep_index] * residual]
  transfers between devices with their start and end apart: 49 -> 0, of which waited for: 48 -> 0; matrix products, arithmetic and copies ran while one was open for 5% -> 0% of each run, Pallas kernels for 0% -> 0%
where the time goes in v1:
time: 83.6 us; the launch traced here: 83.3 us
  Pallas kernels  77.6 us (93%)
  local copies, waits for them, and re-layouts  5.59 us (7%)
    pallas_call x1, Pallas kernels, pair_per_device(): pl.pallas_call(functools.partial(window_kernel, steps, spots, inverse_cen...  77.6 us
    unnamed x25, local copies, waits for them, and re-layouts  5.59 us

profile of v1, /device:TPU:0, one launch (start us, length us, event | category | flops | bytes accessed | tf_op | source)
XLA Modules:
  0.0 83.3 jit_solution(5639938938534107336)
XLA Ops:
  0.0 0.0 copy-start.4
  0.0 0.0 copy-start.9
  0.0 0.0 copy-start.10
  0.0 0.0 copy-start.11
  0.0 0.0 copy-start.6
  0.0 0.0 copy-start.7
  0.0 0.0 copy-start.8
  0.0 0.7 copy-done.4
  0.7 0.0 copy-done.9
  0.7 0.0 copy-done.10
  0.7 0.0 copy-done.11
  0.7 0.0 copy-done.6
  0.7 0.0 copy-done.7
  0.7 0.0 copy-done.8
  0.8 0.0 copy-start
  0.8 1.0 %copy-done = f32[16,3,2,8,128]{4,3,2,1,0:T(8,128)S(1)} copy-done((f32[16,3,2,8,128]{4,3,2,1,0:T(8,128)S(1)}, f32[16,3,2,8,128]{4,3,2,1,0:T(8,128)}, u32[]{:S(2)}) %copy-start) | copy-done | bytes 393240
  1.7 0.0 copy-start.1
  1.8 1.0 %copy-done.1 = f32[16,3,2,8,128]{4,3,2,1,0:T(8,128)S(1)} copy-done((f32[16,3,2,8,128]{4,3,2,1,0:T(8,128)S(1)}, f32[16,3,2,8,128]{4,3,2,1,0:T(8,128)}, u32[]{:S(2)}) %copy-start.1) | copy-done | bytes 393240
  2.7 0.0 copy-start.2
  2.7 0.7 copy-done.2
  3.5 0.7 copy-done.3
  4.2 0.7 copy-done.5
  4.9 77.6 %shard_map.118 = f32[16,6,8,128]{3,2,1,0:T(8,128)S(1)} custom-call(f32[128]{0:T(128)S(1)} %copy-done.11, f32[2048]{0:T(1024)S(1)} %copy-done.5, f32[8]{0:T(128)S(1)} %copy-done.10, f32[128]{0:T(128)S(1)} %copy-done.9, f32[22]{0:T(128)S(1)} %copy-done.8, f32[2048]{0:T(1024)S(1)} %copy-done.4, f32[128]{0:T(128)S(1)} %copy-done.7, f32[3]{0:T(128)S(1)} %copy-done.6, ...), custom_call_target="tpu_custom_call" | custom-call | tf_op jit(solution)/shard_map/pallas_call | solution.py:485
  82.5 0.7 copy.14
  (2 shorter events, 0.0 us)
Async XLA Ops:
  0.0 0.7 copy-start.4
  0.0 0.7 copy-start.9
  0.0 0.7 copy-start.10
  0.0 0.7 copy-start.11
  0.0 0.7 copy-start.6
  0.0 0.7 copy-start.7
  0.0 0.7 copy-start.8
  0.8 1.0 %copy-start = (f32[16,3,2,8,128]{4,3,2,1,0:T(8,128)S(1)}, f32[16,3,2,8,128]{4,3,2,1,0:T(8,128)}, u32[]{:S(2)}) copy-start(f32[16,3,2,8,128]{4,3,2,1,0:T(8,128)} %param.12) | copy-start | bytes 1179652
  1.7 1.0 %copy-start.1 = (f32[16,3,2,8,128]{4,3,2,1,0:T(8,128)S(1)}, f32[16,3,2,8,128]{4,3,2,1,0:T(8,128)}, u32[]{:S(2)}) copy-start(f32[16,3,2,8,128]{4,3,2,1,0:T(8,128)} %param.14) | copy-start | bytes 1179652
  2.7 0.7 copy-start.2
  3.5 0.7 copy-start.3
  4.2 0.7 copy-start.5

commit v2 on v1

--- a/solution.py
+++ b/solution.py
@@ -176,7 +176,7 @@
     return updated.reshape(forcing.shape)
 
 
-CHUNKS = 6
+CHUNKS = 3
 
 
 def pair_numbers(window, groups, spots):
@@ -199,7 +199,6 @@
     split = np.zeros((groups, 2, steps))
     ahead = np.zeros((groups, spots, 2, 2, steps))
     back = np.zeros((groups, 2, steps, spots, 2))
-    last = np.zeros((groups, 2))
     for z in range(groups):
         mine, other = steps * z + rows, steps * ((z + 2) % 4) + rows
         upper = z // 2
@@ -213,8 +212,6 @@
                 for side, low in enumerate((z % 2, 1 - z % 2)):
                     ahead[z, s, f, side] = cas(k, steps * low + rows)
                     back[z, side, :, s, f] = cas(k, steps * low + rows)
-    last[1, 1] = 1.0
-    last[3, 0] = 1.0
     theta = 2 * np.pi * pairs / window
     plain = 1 - gamma * np.cos(theta)
     p_plus = np.where(pairs == 0, 1 - gamma, plain)
@@ -228,14 +225,25 @@
         later = 1.0 / (2.0 * center / radius - now)
         cheb += [later * now, 2.0 * later / radius]
         now = later
-    flat = lambda value: np.asarray(value, np.float32).reshape(-1)
-    return [flat(v) for v in (merge, ahead, last, coef, cheb, back, split)], 1 / center
+    flat = [np.asarray(v, np.float32).reshape(-1) for v in (merge, ahead, coef, cheb, back, split)]
+    offsets = np.cumsum([0] + [v.size for v in flat]).tolist()
+    table = np.zeros(-(-offsets[-1] // 1024) * 1024, np.float32)
+    table[: offsets[-1]] = np.concatenate(flat)
+    return table, offsets, 1 / center
+
+
+class Part:
+    def __init__(self, ref, offset):
+        self.ref, self.offset = ref, offset
+
+    def __getitem__(self, index):
+        return self.ref[index + self.offset]
 
 
 def window_kernel(
-    steps, spots, inverse_center,
-    merge, ahead, last, coef, cheb, back, split, conductance,
-    force, start, region, iterate, out,
+    steps, spots, offsets, inverse_center,
+    conductance, table_hbm, force_hbm, start_hbm, region_hbm, iterate_hbm, out,
+    table, force, start, region, latest, local_sem,
     got_last, got_far, mixed, got_near, extra, got_extra, mine_freq, spec, sigma,
     first, res, step, total, home, half, got_half, even, got_even,
     last_sem, far_sem, near_sem, extra_sem, sigma_sem, spec_sem, home_sem, half_sem, even_sem,
@@ -263,6 +271,17 @@
     for device in [far, near] + peers:
         pl.semaphore_signal(barrier, inc=1, device_id=device, device_id_type=pl.DeviceIdType.MESH)
 
+    local = [
+        pltpu.make_async_copy(source, target, local_sem.at[i])
+        for i, (source, target) in enumerate([
+            (region_hbm, region), (table_hbm, table), (force_hbm, force),
+            (start_hbm, start), (iterate_hbm.at[steps - 1], latest),
+        ])
+    ]
+    for copy in local:
+        copy.start()
+    merge, ahead, coef, cheb, back, split = [Part(table, offset) for offset in offsets[:-1]]
+    local[0].wait()
     material = region[...]
     brick_sigma = jnp.zeros(material.shape, jnp.float32)
     for index in range(3):
@@ -270,16 +289,37 @@
     sigma[s] = brick_sigma
     pl.semaphore_wait(barrier, 2 + len(peers))
 
-    last_copy = send(iterate.at[steps - 1], got_last, last_sem, (0,), far)
+    last_copy = pltpu.make_async_remote_copy(
+        src_ref=iterate_hbm.at[steps - 1], dst_ref=got_last,
+        send_sem=last_sem.at[0], recv_sem=last_sem.at[1],
+        device_id=far, device_id_type=pl.DeviceIdType.MESH,
+    )
+
+    @pl.when(z == 3)
+    def _():
+        last_copy.start()
+
     far_copies = [
-        send(force.at[:, part], got_far.at[:, part], far_sem, (c,), far)
+        send(force_hbm.at[:, part], got_far.at[:, part], far_sem, (c,), far)
         for c, part in enumerate(parts)
     ]
     sigma_copies = [
         send(sigma.at[s], sigma.at[s], sigma_sem, (h,), peer) for h, peer in enumerate(peers)
     ]
-    last_copy.wait_recv()
-    extra[...] = last[z * 2] * iterate[steps - 1] + last[z * 2 + 1] * got_last[...]
+    for copy in local[1:]:
+        copy.wait()
+    extra[...] = jnp.zeros_like(extra)
+
+    @pl.when(z == 1)
+    def _():
+        last_copy.wait_recv()
+        extra[...] = got_last[...]
+
+    @pl.when(z == 3)
+    def _():
+        last_copy.wait_send()
+        extra[...] = latest[...]
+
     extra_copy = send(extra, got_extra, extra_sem, (0,), near)
 
     def mix(c):
@@ -385,15 +425,14 @@
 
     def begin(i, e, f, value):
         at = (i // 2, 2 * e + i % 2, f)
-        g = value * inverse_scale
-        res[at] = g
-        step[at] = g * inverse_center
+        res[at] = value
+        step[at] = value * (inverse_scale * inverse_center)
         total[at] = zero
 
     operator(spec, -1.0, begin)
 
     def sweep(index, carry):
-        w_step, w_res = cheb[index * 2], cheb[index * 2 + 1]
+        w_step, w_res = cheb[index * 2], cheb[index * 2 + 1] * inverse_scale
 
         def keep(i, e, f, value):
             first[i // 2, 2 * e + i % 2, f] = value
@@ -402,7 +441,7 @@
             at = (i // 2, 2 * e + i % 2, f)
             old = step[at]
             total[at] = total[at] + old
-            new = res[at] - value * inverse_scale
+            new = res[at] - value
             res[at] = new
             step[at] = w_step * old + w_res * new
 
@@ -474,7 +513,7 @@
 
 def pair_per_device(groups, spots, forcing, start_field, iterate, region, conductance):
     steps = forcing.shape[0]
-    tables, inverse_center = host_tables(steps * groups, groups, spots)
+    table, offsets, inverse_center = host_tables(steps * groups, groups, spots)
     tile = forcing.shape[3:]
     f32 = jnp.float32
     brick = lambda *lead: pltpu.VMEM(lead + tile, f32)
@@ -482,15 +521,18 @@
     grid = brick(spots, 6, 2)
     dma = pltpu.SemaphoreType.DMA
     smem, vmem = pl.BlockSpec(memory_space=pltpu.SMEM), pl.BlockSpec(memory_space=pltpu.VMEM)
+    hbm = pl.BlockSpec(memory_space=pl.ANY)
     result = pl.pallas_call(
-        functools.partial(window_kernel, steps, spots, inverse_center),
+        functools.partial(window_kernel, steps, spots, offsets, inverse_center),
         out_shape=jax.ShapeDtypeStruct((steps, 6) + tile, f32),
-        in_specs=[smem] * 8 + [vmem] * 4,
+        in_specs=[smem] + [hbm] * 5,
         out_specs=vmem,
         scratch_shapes=[
+            pltpu.SMEM(table.shape, f32), rows, brick(6), pltpu.VMEM(region.shape, region.dtype),
+            brick(6), dma((5,)),
             brick(6), rows, rows, rows, brick(6), brick(6), grid, grid, brick(spots, 2),
             grid, grid, grid, grid, grid, rows, rows, rows, rows,
-            dma((2, 1)), dma((2, CHUNKS)), dma((2, CHUNKS)), dma((2, 1)), dma((2, spots - 1)),
+            dma((2,)), dma((2, CHUNKS)), dma((2, CHUNKS)), dma((2, 1)), dma((2, spots - 1)),
             dma((2, CHUNKS, spots - 1)), dma((2, CHUNKS, spots - 1)),
             dma((2, CHUNKS)), dma((2, CHUNKS)),
         ],
@@ -498,7 +540,7 @@
             collective_id=0, has_side_effects=True, vmem_limit_bytes=32 * 1024 * 1024
         ),
     )(
-        *[jnp.asarray(table) for table in tables], conductance,
+        conductance, jnp.asarray(table),
         forcing.reshape((steps, 6) + tile), start_field.reshape((6,) + tile), region,
         iterate.reshape((steps, 6) + tile),
     )

time: 83.6 us -> 82.4 us (0.986)
  Pallas kernels: 77.6 us -> 76.5 us
    pallas_call x1, Pallas kernels: 77.6 us -> 76.5 us  [pair_per_device(): pl.pallas_call(functools.partial(window_kernel, steps, spots, offsets, in...]
    unnamed x25 -> x13, local copies, waits for them, and re-layouts: 5.59 us -> 5.55 us
where the time goes in v2:
time: 82.4 us; the launch traced here: 82 us
  Pallas kernels  76.5 us (93%)
  local copies, waits for them, and re-layouts  5.55 us (7%)
    pallas_call x1, Pallas kernels, pair_per_device(): pl.pallas_call(functools.partial(window_kernel, steps, spots, offsets, in...  76.5 us
    unnamed x13, local copies, waits for them, and re-layouts  5.55 us

profile of v2, /device:TPU:0, one launch (start us, length us, event | category | flops | bytes accessed | tf_op | source)
XLA Modules:
  0.0 82.0 jit_solution(562414781616996259)
XLA Ops:
  0.0 0.0 copy-start.5
  0.0 0.7 copy-done.5
  0.7 0.0 copy-start
  0.7 1.0 %copy-done = f32[16,3,2,8,128]{4,3,2,1,0:T(8,128)S(1)} copy-done((f32[16,3,2,8,128]{4,3,2,1,0:T(8,128)S(1)}, f32[16,3,2,8,128]{4,3,2,1,0:T(8,128)}, u32[]{:S(2)}) %copy-start) | copy-done | bytes 393240
  1.7 0.0 copy-start.1
  1.7 1.0 %copy-done.1 = f32[16,3,2,8,128]{4,3,2,1,0:T(8,128)S(1)} copy-done((f32[16,3,2,8,128]{4,3,2,1,0:T(8,128)S(1)}, f32[16,3,2,8,128]{4,3,2,1,0:T(8,128)}, u32[]{:S(2)}) %copy-start.1) | copy-done | bytes 393240
  2.6 0.0 copy-start.2
  2.7 0.7 copy-done.2
  3.4 0.0 copy-start.3
  3.4 0.7 copy-done.3
  4.1 0.0 copy-start.4
  4.1 0.7 copy-done.4
  4.8 76.5 %shard_map.64 = f32[16,6,8,128]{3,2,1,0:T(8,128)S(1)} custom-call(f32[3]{0:T(128)S(1)} %copy-done.5, f32[5120]{0:T(1024)S(1)} %copy-done.3, f32[16,6,8,128]{3,2,1,0:T(8,128)S(1)} %bitcast.5, f32[6,8,128]{2,1,0:T(8,128)S(1)} %bitcast.7, s32[2,8,128]{2,1,0:T(8,128)S(1)} %copy-done.4, f32[16,6,8,128]{3,2,1,0:T(8,128)S(1)} %bitcast.6), custom_call_target="tpu_custom_call" | custom-call | tf_op jit(solution)/shard_map/pallas_call | solution.py:525
  81.3 0.7 copy.8
Async XLA Ops:
  0.0 0.7 copy-start.5
  0.7 1.0 %copy-start = (f32[16,3,2,8,128]{4,3,2,1,0:T(8,128)S(1)}, f32[16,3,2,8,128]{4,3,2,1,0:T(8,128)}, u32[]{:S(2)}) copy-start(f32[16,3,2,8,128]{4,3,2,1,0:T(8,128)} %param.6) | copy-start | bytes 1179652
  1.7 1.0 %copy-start.1 = (f32[16,3,2,8,128]{4,3,2,1,0:T(8,128)S(1)}, f32[16,3,2,8,128]{4,3,2,1,0:T(8,128)}, u32[]{:S(2)}) copy-start(f32[16,3,2,8,128]{4,3,2,1,0:T(8,128)} %param.8) | copy-start | bytes 1179652
  2.6 0.7 copy-start.2
  3.4 0.7 copy-start.3
  4.1 0.7 copy-start.4

commit v3 on v2

--- a/solution.py
+++ b/solution.py
@@ -176,7 +176,9 @@
     return updated.reshape(forcing.shape)
 
 
-CHUNKS = 3
+VMEM_BYTES = 63 * 1024 * 1024
+AHEAD = 2
+CHUNKS = 6
 
 
 def pair_numbers(window, groups, spots):
@@ -242,8 +244,8 @@
 
 def window_kernel(
     steps, spots, offsets, inverse_center,
-    conductance, table_hbm, force_hbm, start_hbm, region_hbm, iterate_hbm, out,
-    table, force, start, region, latest, local_sem,
+    conductance_hbm, table_hbm, force_hbm, start_hbm, region_hbm, iterate_hbm, out_hbm,
+    out, out_sem, conductance, table, force, start, region, latest, local_sem,
     got_last, got_far, mixed, got_near, extra, got_extra, mine_freq, spec, sigma,
     first, res, step, total, home, half, got_half, even, got_even,
     last_sem, far_sem, near_sem, extra_sem, sigma_sem, spec_sem, home_sem, half_sem, even_sem,
@@ -274,7 +276,7 @@
     local = [
         pltpu.make_async_copy(source, target, local_sem.at[i])
         for i, (source, target) in enumerate([
-            (region_hbm, region), (table_hbm, table), (force_hbm, force),
+            (region_hbm, region), (conductance_hbm, conductance), (table_hbm, table), (force_hbm, force),
             (start_hbm, start), (iterate_hbm.at[steps - 1], latest),
         ])
     ]
@@ -282,6 +284,7 @@
         copy.start()
     merge, ahead, coef, cheb, back, split = [Part(table, offset) for offset in offsets[:-1]]
     local[0].wait()
+    local[1].wait()
     material = region[...]
     brick_sigma = jnp.zeros(material.shape, jnp.float32)
     for index in range(3):
@@ -299,14 +302,22 @@
     def _():
         last_copy.start()
 
-    far_copies = [
-        send(force_hbm.at[:, part], got_far.at[:, part], far_sem, (c,), far)
-        for c, part in enumerate(parts)
-    ]
+    far_copies = []
+
+    def send_far():
+        c = len(far_copies)
+        if c < CHUNKS:
+            part = parts[c]
+            far_copies.append(
+                send(force_hbm.at[:, part], got_far.at[:, part], far_sem, (c,), far)
+            )
+
+    for _ in range(AHEAD):
+        send_far()
     sigma_copies = [
         send(sigma.at[s], sigma.at[s], sigma_sem, (h,), peer) for h, peer in enumerate(peers)
     ]
-    for copy in local[1:]:
+    for copy in local[2:]:
         copy.wait()
     extra[...] = jnp.zeros_like(extra)
 
@@ -324,6 +335,7 @@
 
     def mix(c):
         far_copies[c].wait_recv()
+        send_far()
 
         def row(m, carry):
             w_mine, w_other = merge[z * 2 * steps + m], merge[(z * 2 + 1) * steps + m]
@@ -452,7 +464,12 @@
     lax.fori_loop(0, SWEEPS - 1, sweep, 0)
 
     home_copies = []
-    for c, part in enumerate(parts):
+
+    def send_home():
+        c = len(home_copies)
+        if c == CHUNKS:
+            return
+        part = parts[c]
         for b in range(spots):
             for t in range(c * width, (c + 1) * width):
                 for f in range(2):
@@ -491,11 +508,15 @@
         even[:, parts[c]] = even[:, parts[c]] + got_half[:, parts[c]]
         return send(even.at[:, parts[c]], got_even.at[:, parts[c]], even_sem, (c,), far)
 
+    send_home()
+    send_home()
     half_copies = [gather(0)]
-    even_copies = []
+    send_home()
+    even_copies, out_copies = [], []
     for c in range(CHUNKS):
         if c + 1 < CHUNKS:
             half_copies.append(gather(c + 1))
+            send_home()
         even_copies.append(add(c, half_copies[c]))
     for c in range(CHUNKS):
         even_copies[c].wait_recv()
@@ -507,8 +528,14 @@
             return carry
 
         lax.fori_loop(0, steps, row, 0, unroll=4)
+        out_copies.append(
+            pltpu.make_async_copy(out.at[:, parts[c]], out_hbm.at[:, parts[c]], out_sem.at[c])
+        )
+        out_copies[c].start()
     for copy in sent:
         copy.wait_send()
+    for copy in out_copies:
+        copy.wait()
 
 
 def pair_per_device(groups, spots, forcing, start_field, iterate, region, conductance):
@@ -520,16 +547,15 @@
     rows = brick(steps, 6)
     grid = brick(spots, 6, 2)
     dma = pltpu.SemaphoreType.DMA
-    smem, vmem = pl.BlockSpec(memory_space=pltpu.SMEM), pl.BlockSpec(memory_space=pltpu.VMEM)
     hbm = pl.BlockSpec(memory_space=pl.ANY)
     result = pl.pallas_call(
         functools.partial(window_kernel, steps, spots, offsets, inverse_center),
         out_shape=jax.ShapeDtypeStruct((steps, 6) + tile, f32),
-        in_specs=[smem] + [hbm] * 5,
-        out_specs=vmem,
+        in_specs=[hbm] * 6,
+        out_specs=hbm,
         scratch_shapes=[
-            pltpu.SMEM(table.shape, f32), rows, brick(6), pltpu.VMEM(region.shape, region.dtype),
-            brick(6), dma((5,)),
+            rows, dma((CHUNKS,)), pltpu.SMEM(conductance.shape, f32), pltpu.SMEM(table.shape, f32), rows, brick(6), pltpu.VMEM(region.shape, region.dtype),
+            brick(6), dma((6,)),
             brick(6), rows, rows, rows, brick(6), brick(6), grid, grid, brick(spots, 2),
             grid, grid, grid, grid, grid, rows, rows, rows, rows,
             dma((2,)), dma((2, CHUNKS)), dma((2, CHUNKS)), dma((2, 1)), dma((2, spots - 1)),
@@ -537,7 +563,7 @@
             dma((2, CHUNKS)), dma((2, CHUNKS)),
         ],
         compiler_params=pltpu.CompilerParams(
-            collective_id=0, has_side_effects=True, vmem_limit_bytes=32 * 1024 * 1024
+            collective_id=0, has_side_effects=True, vmem_limit_bytes=VMEM_BYTES
         ),
     )(
         conductance, jnp.asarray(table),

time: 82.4 us -> 77.5 us (0.941)
  local copies, waits for them, and re-layouts: 5.55 us -> 1.77 us
  Pallas kernels: 76.5 us -> 75.6 us
    unnamed x13 -> x1, local copies, waits for them, and re-layouts: 5.55 us -> 1.77 us
    pallas_call x1, Pallas kernels: 76.5 us -> 75.6 us  [pair_per_device(): pl.pallas_call(functools.partial(window_kernel, steps, spots, offsets, in...]
where the time goes in v3:
time: 77.5 us; the launch traced here: 77.3 us
  Pallas kernels  75.6 us (98%)
  local copies, waits for them, and re-layouts  1.77 us (2%)
    pallas_call x1, Pallas kernels, pair_per_device(): pl.pallas_call(functools.partial(window_kernel, steps, spots, offsets, in...  75.6 us
    unnamed x1, local copies, waits for them, and re-layouts  1.77 us

profile of v3, /device:TPU:0, one launch (start us, length us, event | category | flops | bytes accessed | tf_op | source)
XLA Modules:
  0.0 77.3 jit_solution(2334668913151662673)
XLA Ops:
  0.0 75.6 %shard_map.64 = f32[16,6,8,128]{3,2,1,0:T(8,128)} custom-call(f32[3]{0:T(128)} %conductance_hbm.1, f32[5120]{0:T(1024)} %constant.2.clone.table_hbm, f32[16,6,8,128]{3,2,1,0:T(8,128)} %bitcast.5, f32[6,8,128]{2,1,0:T(8,128)} %bitcast.7, s32[2,8,128]{2,1,0:T(8,128)} %region_hbm.1, f32[16,6,8,128]{3,2,1,0:T(8,128)} %bitcast.6), custom_call_target="tpu_custom_call" | custom-call | tf_op jit(solution)/shard_map/pallas_call | solution.py:551
  75.6 1.8 %copy.8 = f32[16,3,2,8,128]{4,3,2,1,0:T(8,128)} copy(f32[16,3,2,8,128]{4,3,2,1,0:T(8,128)} %bitcast.4) | data formatting | bytes 786432

commit v4 on v3

--- a/solution.py
+++ b/solution.py
@@ -276,8 +276,9 @@
     local = [
         pltpu.make_async_copy(source, target, local_sem.at[i])
         for i, (source, target) in enumerate([
-            (region_hbm, region), (conductance_hbm, conductance), (table_hbm, table), (force_hbm, force),
+            (region_hbm, region), (conductance_hbm, conductance), (table_hbm, table),
             (start_hbm, start), (iterate_hbm.at[steps - 1], latest),
+            *[(force_hbm.at[:, i], force.at[i]) for i in range(6)],
         ])
     ]
     for copy in local:
@@ -308,16 +309,16 @@
         c = len(far_copies)
         if c < CHUNKS:
             part = parts[c]
-            far_copies.append(
-                send(force_hbm.at[:, part], got_far.at[:, part], far_sem, (c,), far)
-            )
+            for copy in local[5 + c * width : 5 + (c + 1) * width]:
+                copy.wait()
+            far_copies.append(send(force.at[part], got_far.at[part], far_sem, (c,), far))
 
     for _ in range(AHEAD):
         send_far()
     sigma_copies = [
         send(sigma.at[s], sigma.at[s], sigma_sem, (h,), peer) for h, peer in enumerate(peers)
     ]
-    for copy in local[2:]:
+    for copy in local[2:5]:
         copy.wait()
     extra[...] = jnp.zeros_like(extra)
 
@@ -340,11 +341,11 @@
         def row(m, carry):
             w_mine, w_other = merge[z * 2 * steps + m], merge[(z * 2 + 1) * steps + m]
             for t in range(c * width, (c + 1) * width):
-                mixed[m, t] = w_mine * force[m, t] + w_other * got_far[m, t]
+                mixed[t, m] = w_mine * force[t, m] + w_other * got_far[t, m]
             return carry
 
         lax.fori_loop(0, steps, row, 0, unroll=4)
-        return send(mixed.at[:, parts[c]], got_near.at[:, parts[c]], near_sem, (c,), near)
+        return send(mixed.at[parts[c]], got_near.at[parts[c]], near_sem, (c,), near)
 
     spec_copies = [None] * CHUNKS
 
@@ -362,14 +363,14 @@
                 w_mine, w_other = ahead[base + m], ahead[base + steps + m]
                 for i in range(width):
                     t = c * width + i
-                    term = w_other * got_near[m, t]
-                    sums[i][0] = sums[i][0] + w_mine * mixed[m, t]
+                    term = w_other * got_near[t, m]
+                    sums[i][0] = sums[i][0] + w_mine * mixed[t, m]
                     sums[i][1] = term if m == 0 else sums[i][1] + term
             for i in range(width):
                 mine_freq[k // 2, c * width + i, k % 2] = sums[i][0] + sums[i][1]
             return carry
 
-        lax.fori_loop(0, 2 * spots, slot, 0)
+        lax.fori_loop(0, 2 * spots, slot, 0, unroll=4)
         spec[s, parts[c]] = mine_freq[s, parts[c]]
         spec_copies[c] = [
             send(mine_freq.at[peer[1], parts[c]], spec.at[s, parts[c]], spec_sem, (c, h), peer)
@@ -488,25 +489,25 @@
             base_mine = (z * 2 * steps + m) * 2 * spots
             base_other = ((z * 2 + 1) * steps + m) * 2 * spots
             for t in range(c * width, (c + 1) * width):
-                mine, other = None, None
+                mine, other = [None, None], [None, None]
                 for b in range(spots):
                     for f in range(2):
                         value = home[b, t, f]
                         term = back[base_mine + 2 * b + f] * value
-                        mine = term if mine is None else mine + term
+                        mine[f] = term if b == 0 else mine[f] + term
                         term = back[base_other + 2 * b + f] * value
-                        other = term if other is None else other + term
-                even[m, t] = mine
-                half[m, t] = other
+                        other[f] = term if b == 0 else other[f] + term
+                even[t, m] = mine[0] + mine[1]
+                half[t, m] = other[0] + other[1]
             return carry
 
-        lax.fori_loop(0, steps, row, 0)
-        return send(half.at[:, parts[c]], got_half.at[:, parts[c]], half_sem, (c,), near)
+        lax.fori_loop(0, steps, row, 0, unroll=4)
+        return send(half.at[parts[c]], got_half.at[parts[c]], half_sem, (c,), near)
 
     def add(c, copy):
         copy.wait_recv()
-        even[:, parts[c]] = even[:, parts[c]] + got_half[:, parts[c]]
-        return send(even.at[:, parts[c]], got_even.at[:, parts[c]], even_sem, (c,), far)
+        even[parts[c]] = even[parts[c]] + got_half[parts[c]]
+        return send(even.at[parts[c]], got_even.at[parts[c]], even_sem, (c,), far)
 
     send_home()
     send_home()
@@ -524,14 +525,13 @@
         def row(m, carry):
             w_mine, w_other = split[z * 2 * steps + m], split[(z * 2 + 1) * steps + m]
             for t in range(c * width, (c + 1) * width):
-                out[m, t] = w_mine * even[m, t] + w_other * got_even[m, t]
+                out[t, m] = w_mine * even[t, m] + w_other * got_even[t, m]
             return carry
 
         lax.fori_loop(0, steps, row, 0, unroll=4)
-        out_copies.append(
-            pltpu.make_async_copy(out.at[:, parts[c]], out_hbm.at[:, parts[c]], out_sem.at[c])
-        )
-        out_copies[c].start()
+        for t in range(c * width, (c + 1) * width):
+            out_copies.append(pltpu.make_async_copy(out.at[t], out_hbm.at[:, t], out_sem.at[t]))
+            out_copies[t].start()
     for copy in sent:
         copy.wait_send()
     for copy in out_copies:
@@ -544,7 +544,7 @@
     tile = forcing.shape[3:]
     f32 = jnp.float32
     brick = lambda *lead: pltpu.VMEM(lead + tile, f32)
-    rows = brick(steps, 6)
+    rows = brick(6, steps)
     grid = brick(spots, 6, 2)
     dma = pltpu.SemaphoreType.DMA
     hbm = pl.BlockSpec(memory_space=pl.ANY)
@@ -554,8 +554,8 @@
         in_specs=[hbm] * 6,
         out_specs=hbm,
         scratch_shapes=[
-            rows, dma((CHUNKS,)), pltpu.SMEM(conductance.shape, f32), pltpu.SMEM(table.shape, f32), rows, brick(6), pltpu.VMEM(region.shape, region.dtype),
-            brick(6), dma((6,)),
+            rows, dma((6,)), pltpu.SMEM(conductance.shape, f32), pltpu.SMEM(table.shape, f32), rows, brick(6), pltpu.VMEM(region.shape, region.dtype),
+            brick(6), dma((11,)),
             brick(6), rows, rows, rows, brick(6), brick(6), grid, grid, brick(spots, 2),
             grid, grid, grid, grid, grid, rows, rows, rows, rows,
             dma((2,)), dma((2, CHUNKS)), dma((2, CHUNKS)), dma((2, 1)), dma((2, spots - 1)),

time: 77.5 us -> 76.9 us (level)
  no operation moved by 1% of the time
where the time goes in v4:
time: 76.9 us; the launch traced here: 76.8 us
  Pallas kernels  75 us (98%)
  local copies, waits for them, and re-layouts  1.77 us (2%)
    pallas_call x1, Pallas kernels, pair_per_device(): pl.pallas_call(functools.partial(window_kernel, steps, spots, offsets, in...  75 us
    unnamed x1, local copies, waits for them, and re-layouts  1.77 us

profile of v4, /device:TPU:0, one launch (start us, length us, event | category | flops | bytes accessed | tf_op | source)
XLA Modules:
  0.0 76.8 jit_solution(11734793383509761696)
XLA Ops:
  0.0 75.0 %shard_map.64 = f32[16,6,8,128]{3,2,1,0:T(8,128)} custom-call(f32[3]{0:T(128)} %conductance_hbm.1, f32[5120]{0:T(1024)} %constant.2.clone.table_hbm, f32[16,6,8,128]{3,2,1,0:T(8,128)} %bitcast.5, f32[6,8,128]{2,1,0:T(8,128)} %bitcast.7, s32[2,8,128]{2,1,0:T(8,128)} %region_hbm.1, f32[16,6,8,128]{3,2,1,0:T(8,128)} %bitcast.6), custom_call_target="tpu_custom_call" | custom-call | tf_op jit(solution)/shard_map/pallas_call | solution.py:551
  75.0 1.8 %copy.8 = f32[16,3,2,8,128]{4,3,2,1,0:T(8,128)} copy(f32[16,3,2,8,128]{4,3,2,1,0:T(8,128)} %bitcast.4) | data formatting | bytes 786432

commit v5 on v4

--- a/solution.py
+++ b/solution.py
@@ -177,7 +177,7 @@
 
 
 VMEM_BYTES = 63 * 1024 * 1024
-AHEAD = 2
+AHEAD = 3
 CHUNKS = 6
 
 
@@ -247,7 +247,7 @@
     conductance_hbm, table_hbm, force_hbm, start_hbm, region_hbm, iterate_hbm, out_hbm,
     out, out_sem, conductance, table, force, start, region, latest, local_sem,
     got_last, got_far, mixed, got_near, extra, got_extra, mine_freq, spec, sigma,
-    first, res, step, total, home, half, got_half, even, got_even,
+    res, step, total, home, half, got_half, even, got_even,
     last_sem, far_sem, near_sem, extra_sem, sigma_sem, spec_sem, home_sem, half_sem, even_sem,
 ):
     z, s = lax.axis_index("tm"), lax.axis_index("space")
@@ -406,8 +406,12 @@
     def down_z(v):
         return jnp.where(not_low_z, pltpu.roll(v, 1, 1), 0.0)
 
-    def operator(buffer, sign, finish):
-        load = lambda i: [[buffer[i // 2, 2 * e + i % 2, f] for e in range(3)] for f in range(2)]
+    def planes_of(buffer):
+        return lambda i: [
+            [buffer[i // 2, 2 * e + i % 2, f] for e in range(3)] for f in range(2)
+        ]
+
+    def operator(load, sign, finish):
         here = load(0)
         behind = [(zero, zero), (zero, zero)]
         for i in range(planes):
@@ -435,6 +439,7 @@
                     value = value + swapped if (f == 1) == (sign > 0) else value - swapped
                     finish(i, e, f, value)
             here = ahead_field
+            yield
 
     def begin(i, e, f, value):
         at = (i // 2, 2 * e + i % 2, f)
@@ -442,13 +447,16 @@
         step[at] = value * (inverse_scale * inverse_center)
         total[at] = zero
 
-    operator(spec, -1.0, begin)
+    for _ in operator(planes_of(spec), -1.0, begin):
+        pass
 
     def sweep(index, carry):
         w_step, w_res = cheb[index * 2], cheb[index * 2 + 1] * inverse_scale
 
+        first = [[[None] * 3 for _ in range(2)] for _ in range(planes)]
+
         def keep(i, e, f, value):
-            first[i // 2, 2 * e + i % 2, f] = value
+            first[i][f][e] = value
 
         def advance(i, e, f, value):
             at = (i // 2, 2 * e + i % 2, f)
@@ -458,8 +466,13 @@
             res[at] = new
             step[at] = w_step * old + w_res * new
 
-        operator(step, 1.0, keep)
-        operator(first, -1.0, advance)
+        ahead_pass = operator(planes_of(step), 1.0, keep)
+        behind_pass = operator(lambda i: first[i], -1.0, advance)
+        next(ahead_pass)
+        for _ in range(planes - 1):
+            next(ahead_pass)
+            next(behind_pass)
+        next(behind_pass)
         return carry
 
     lax.fori_loop(0, SWEEPS - 1, sweep, 0)
@@ -557,7 +570,7 @@
             rows, dma((6,)), pltpu.SMEM(conductance.shape, f32), pltpu.SMEM(table.shape, f32), rows, brick(6), pltpu.VMEM(region.shape, region.dtype),
             brick(6), dma((11,)),
             brick(6), rows, rows, rows, brick(6), brick(6), grid, grid, brick(spots, 2),
-            grid, grid, grid, grid, grid, rows, rows, rows, rows,
+            grid, grid, grid, grid, rows, rows, rows, rows,
             dma((2,)), dma((2, CHUNKS)), dma((2, CHUNKS)), dma((2, 1)), dma((2, spots - 1)),
             dma((2, CHUNKS, spots - 1)), dma((2, CHUNKS, spots - 1)),
             dma((2, CHUNKS)), dma((2, CHUNKS)),

time: 76.9 us -> 69.4 us (0.902)
  Pallas kernels: 75 us -> 67.4 us
    pallas_call x1, Pallas kernels: 75 us -> 67.4 us  [pair_per_device(): pl.pallas_call(functools.partial(window_kernel, steps, spots, offsets, in...]
where the time goes in v5:
time: 69.4 us; the launch traced here: 69.2 us
  Pallas kernels  67.4 us (97%)
  local copies, waits for them, and re-layouts  1.77 us (3%)
    pallas_call x1, Pallas kernels, pair_per_device(): pl.pallas_call(functools.partial(window_kernel, steps, spots, offsets, in...  67.4 us
    unnamed x1, local copies, waits for them, and re-layouts  1.77 us

profile of v5, /device:TPU:0, one launch (start us, length us, event | category | flops | bytes accessed | tf_op | source)
XLA Modules:
  0.0 69.2 jit_solution(10891109967497190173)
XLA Ops:
  0.0 67.4 %shard_map.64 = f32[16,6,8,128]{3,2,1,0:T(8,128)} custom-call(f32[3]{0:T(128)} %conductance_hbm.1, f32[5120]{0:T(1024)} %constant.2.clone.table_hbm, f32[16,6,8,128]{3,2,1,0:T(8,128)} %bitcast.5, f32[6,8,128]{2,1,0:T(8,128)} %bitcast.7, s32[2,8,128]{2,1,0:T(8,128)} %region_hbm.1, f32[16,6,8,128]{3,2,1,0:T(8,128)} %bitcast.6), custom_call_target="tpu_custom_call" | custom-call | tf_op jit(solution)/shard_map/pallas_call | solution.py:564
  67.5 1.8 %copy.8 = f32[16,3,2,8,128]{4,3,2,1,0:T(8,128)} copy(f32[16,3,2,8,128]{4,3,2,1,0:T(8,128)} %bitcast.4) | data formatting | bytes 786432

commit v6 on v5

--- a/solution.py
+++ b/solution.py
@@ -444,15 +444,15 @@
     def begin(i, e, f, value):
         at = (i // 2, 2 * e + i % 2, f)
         res[at] = value
-        step[at] = value * (inverse_scale * inverse_center)
-        total[at] = zero
+        moved = value * (inverse_scale * inverse_center)
+        step[at] = moved
+        total[at] = moved
 
     for _ in operator(planes_of(spec), -1.0, begin):
         pass
 
-    def sweep(index, carry):
+    def sweep_passes(index):
         w_step, w_res = cheb[index * 2], cheb[index * 2 + 1] * inverse_scale
-
         first = [[[None] * 3 for _ in range(2)] for _ in range(planes)]
 
         def keep(i, e, f, value):
@@ -460,22 +460,31 @@
 
         def advance(i, e, f, value):
             at = (i // 2, 2 * e + i % 2, f)
-            old = step[at]
-            total[at] = total[at] + old
             new = res[at] - value
             res[at] = new
-            step[at] = w_step * old + w_res * new
-
-        ahead_pass = operator(planes_of(step), 1.0, keep)
-        behind_pass = operator(lambda i: first[i], -1.0, advance)
-        next(ahead_pass)
-        for _ in range(planes - 1):
-            next(ahead_pass)
-            next(behind_pass)
-        next(behind_pass)
+            moved = w_step * step[at] + w_res * new
+            step[at] = moved
+            total[at] = total[at] + moved
+
+        return [
+            operator(planes_of(step), 1.0, keep),
+            operator(lambda i: first[i], -1.0, advance),
+        ]
+
+    def sweeps(indices):
+        passes = [one for index in indices for one in sweep_passes(index)]
+        for tick in range(planes + len(passes) - 1):
+            for lag, one in enumerate(passes):
+                if 0 <= tick - lag < planes:
+                    next(one)
+
+    def two_sweeps(index, carry):
+        sweeps([2 * index, 2 * index + 1])
         return carry
 
-    lax.fori_loop(0, SWEEPS - 1, sweep, 0)
+    lax.fori_loop(0, (SWEEPS - 1) // 2, two_sweeps, 0)
+    if (SWEEPS - 1) % 2:
+        sweeps([SWEEPS - 2])
 
     home_copies = []
 
@@ -484,10 +493,6 @@
         if c == CHUNKS:
             return
         part = parts[c]
-        for b in range(spots):
-            for t in range(c * width, (c + 1) * width):
-                for f in range(2):
-                    total[b, t, f] = total[b, t, f] + step[b, t, f]
         home[s, part] = total[s, part]
         home_copies.append([
             send(total.at[peer[1], part], home.at[s, part], home_sem, (c, h), peer)

time: 69.4 us -> 69.1 us (level)
  no operation moved by 1% of the time
where the time goes in v6:
time: 69.1 us; the launch traced here: 69 us
  Pallas kernels  67.2 us (97%)
  local copies, waits for them, and re-layouts  1.77 us (3%)
    pallas_call x1, Pallas kernels, pair_per_device(): pl.pallas_call(functools.partial(window_kernel, steps, spots, offsets, in...  67.2 us
    unnamed x1, local copies, waits for them, and re-layouts  1.77 us

profile of v6, /device:TPU:0, one launch (start us, length us, event | category | flops | bytes accessed | tf_op | source)
XLA Modules:
  0.0 69.0 jit_solution(3339124491634501694)
XLA Ops:
  0.0 67.2 %shard_map.64 = f32[16,6,8,128]{3,2,1,0:T(8,128)} custom-call(f32[3]{0:T(128)} %conductance_hbm.1, f32[5120]{0:T(1024)} %constant.2.clone.table_hbm, f32[16,6,8,128]{3,2,1,0:T(8,128)} %bitcast.5, f32[6,8,128]{2,1,0:T(8,128)} %bitcast.7, s32[2,8,128]{2,1,0:T(8,128)} %region_hbm.1, f32[16,6,8,128]{3,2,1,0:T(8,128)} %bitcast.6), custom_call_target="tpu_custom_call" | custom-call | tf_op jit(solution)/shard_map/pallas_call | solution.py:569
  67.2 1.8 %copy.8 = f32[16,3,2,8,128]{4,3,2,1,0:T(8,128)} copy(f32[16,3,2,8,128]{4,3,2,1,0:T(8,128)} %bitcast.4) | data formatting | bytes 786432
